TPU v7x, 128 devices: a whole 4x4x4 slice. The times are simulated.
128 devices in a mesh: ray: 16 (over x, y), brick: 8 (over z, core).
Axes of the slice: x: 4, y: 4, z: 4, core: 2. Of those that a mesh axis runs over, the one named last changes fastest.
Arguments:
- estimate: float32 [4, 8192, 128], P(None, ('ray', 'brick')), may hold values from -6 to 6
- blocks: bfloat16 [8, 256, 128, 4096], P('brick', 'ray'), may hold values from -0.0625 to 0.0625
- block_bundle: int32 [8, 256], P('brick', 'ray'), may hold values from 0 to 127
- sinogram: float32 [8, 128, 4, 128], P('brick', 'ray'), may hold values from -6 to 6
Outputs:
- restored: float32 [4, 8192, 128], P(None, ('ray', 'brick'))
- residual: float32 [8, 128, 4, 128], P('brick', 'ray')
All inputs are finite; a program needn't handle non-finite values.
Results may differ from a plain program's by a relative error of at most 0.0031.
Values may be sent and summed in bfloat16 or wider, within the bound.
A program may use at most 64 MiB of HBM per device.

v0:
```python
import jax
import jax.numpy as jnp
from jax import lax
from jax.sharding import PartitionSpec as P

TSIDE = 64
BUNDLES = 128
BCOLS = 2
SWEEPS = 3


step_size = 0.5
tv_step = 0.28
tv_weight = 0.5


def from_everyone(array, axis):
    peers = lax.axis_size(axis)
    return lax.all_to_all(
        jnp.broadcast_to(array[None], (peers, *array.shape)), axis, 0, 0, tiled=True
    )


def laid_out(blocks, dim):
    dims = list(blocks.shape[1:])
    dims[dim] *= blocks.shape[0]
    return jnp.moveaxis(blocks, 0, dim).reshape(dims)


def collect(array, axis, dim):
    blocks = from_everyone(array, axis)
    return laid_out(blocks, dim)


def cut_along(array, dim, peers):
    before, after = (array.shape[:dim], array.shape[dim + 1 :])
    return jnp.moveaxis(array.reshape(*before, peers, -1, *after), dim, 0)


def sent_and_summed(array, axis, dim):
    blocks = cut_along(array, dim, lax.axis_size(axis))
    arrived = lax.all_to_all(blocks, axis, split_axis=0, concat_axis=0, tiled=True)
    return arrived.astype(jnp.float32).sum(axis=0)


def padded_2(array, sides, width):
    edges = {}
    for axis, dim in sides:
        peers, length = (lax.axis_size(axis), array.shape[dim])
        up = [(i, (i + 1) % peers) for i in range(peers - 1)]
        last = lax.slice_in_dim(array, length - width, length, axis=dim)
        initial = lax.slice_in_dim(array, 0, width, axis=dim)
        edges[dim] = (
            lax.ppermute(last, axis, up),
            lax.ppermute(initial, axis, [(b, a) for a, b in up]),
        )
    done = []
    for _, dim in sides:
        low, high = edges[dim]
        around = [(width, width) if d in done else (0, 0) for d in range(array.ndim)]
        array = jnp.concatenate([jnp.pad(low, around), array, jnp.pad(high, around)], axis=dim)
        done.append(dim)
    return array


def local_diffs(field):
    diff_x = jnp.concatenate([field[:, :, 1:], jnp.zeros_like(field[:, :, :1])], axis=2) - field
    diff_z = jnp.concatenate([field[1:] - field[:-1], jnp.zeros_like(field[:1])], axis=0)
    return (diff_x, diff_z)


def dual_update(dual_y, dual_x, dual_z, diff_y, diff_x, diff_z):
    trial_y = dual_y + tv_step * diff_y
    trial_x = dual_x + tv_step * diff_x
    trial_z = dual_z + tv_step * diff_z
    shrink = jnp.sqrt(
        jnp.maximum(
            1.0,
            (trial_y * trial_y + trial_x * trial_x + trial_z * trial_z) / (tv_weight * tv_weight),
        )
    )
    return (trial_y / shrink, trial_x / shrink, trial_z / shrink)


def shards(estimate, blocks, block_bundle, sinogram):
    slices, rows_dev, width = estimate.shape
    band_rows = collect(estimate.astype(jnp.bfloat16), "brick", 1)
    tile_rows = band_rows.shape[1] // TSIDE
    tile_values = band_rows.reshape(slices, tile_rows, TSIDE, BCOLS, TSIDE).transpose(1, 3, 0, 2, 4)
    tile_values = tile_values.reshape(tile_rows * BCOLS, slices, TSIDE * TSIDE)
    contrib = jnp.einsum("tsp,atrp->atsr", tile_values, blocks, preferred_element_type=jnp.float32)
    labels = jnp.arange(BUNDLES, dtype=jnp.int32)
    matches = block_bundle[:, None, :] == labels[None, :, None]
    projected = jnp.einsum(
        "abt,atsr->absr", matches.astype(jnp.float32), contrib, precision=lax.Precision.HIGHEST
    )
    partial_value = sent_and_summed(projected.astype(jnp.bfloat16), "ray", 1)
    residual = partial_value - sinogram
    rounded = collect(residual.astype(jnp.bfloat16), "ray", 1)
    lookup = jnp.einsum(
        "abt,absr->atsr", matches.astype(jnp.bfloat16), rounded, preferred_element_type=jnp.float32
    ).astype(jnp.bfloat16)
    grad_tiles = jnp.einsum("atsr,atrp->tsp", lookup, blocks, preferred_element_type=jnp.float32)
    grad_tiles = grad_tiles.reshape(tile_rows, BCOLS, slices, TSIDE, TSIDE)
    gradient = sent_and_summed(grad_tiles.astype(jnp.bfloat16), "brick", 0)
    grad_image = gradient.transpose(2, 0, 3, 1, 4).reshape(slices, rows_dev, width)
    anchor = estimate - step_size * grad_image
    primal = anchor
    extrapolated = anchor
    dual_y = jnp.zeros_like(anchor)
    dual_x = jnp.zeros_like(anchor)
    dual_z = jnp.zeros_like(anchor)
    for sweep in range(SWEEPS):
        stacked = jnp.stack([extrapolated, dual_y, dual_x, dual_z])
        padded = padded_2(stacked.astype(jnp.bfloat16), ((("ray", "brick"), 2),), 1).astype(
            stacked.dtype
        )
        upper = padded[0]
        field = upper[:, :-1, :]
        diff_y = upper[:, 1:, :] - field
        diff_x, diff_z = local_diffs(field)
        new_y, new_x, new_z = dual_update(
            padded[1, :, :-1, :], padded[2, :, :-1, :], padded[3, :, :-1, :], diff_y, diff_x, diff_z
        )
        inside = jnp.where(lax.axis_index(("ray", "brick")) > 0, 1.0, 0.0)
        above = new_y[:, 0, :] * inside
        dual_y = new_y[:, 1:, :]
        dual_x = new_x[:, 1:, :]
        dual_z = new_z[:, 1:, :]
        part_y = dual_y - jnp.concatenate([above[:, None, :], dual_y[:, :-1, :]], axis=1)
        part_x = dual_x - jnp.concatenate(
            [jnp.zeros_like(dual_x[:, :, :1]), dual_x[:, :, :-1]], axis=2
        )
        part_z = dual_z - jnp.concatenate([jnp.zeros_like(dual_z[:1]), dual_z[:-1]], axis=0)
        updated = (primal + tv_step * (part_y + part_x + part_z) + tv_step * anchor) / (
            1.0 + tv_step
        )
        extrapolated = 2.0 * updated - primal
        primal = updated
    return (primal, residual)


def solution(mesh):
    return jax.shard_map(
        shards,
        mesh=mesh,
        in_specs=(
            P(None, ("ray", "brick"), None),
            P("brick", "ray", None, None),
            P("brick", "ray"),
            P("brick", "ray", None, None),
        ),
        out_specs=(P(None, ("ray", "brick"), None), P("brick", "ray", None, None)),
        check_vma=False,
    )
```

profile of v0, /device:TPU:121, one launch (start us, length us, event | category | flops | bytes accessed | tf_op | source)
XLA Modules:
  0.0 112.3 jit_solution(4117291599734038946)
XLA Ops:
  0.6 0.9 convert_element_type.47
  1.5 0.1 broadcast_in_dim.6
  1.7 12.3 %all_to_all.20 = bf16[8,4,64,128]{3,2,1,0:T(8,128)(2,1)S(1)} all-to-all(bf16[8,4,64,128]{3,2,1,0:T(8,128)(2,1)S(1)} %broadcast_in_dim.6), channel_id=1, replica_groups=mesh['ray'=16,'brick'=8] {'brick'}, dimensions={0} | all-to-all | bytes 1048576 | tf_op jit(solution)/shard_map/all_to_all | solution.py:19
  14.0 0.4 reshape_reshape.3
  14.4 0.0 copy-start.2
  14.4 0.3 copy.31
  14.7 0.0 copy-start.1
  14.7 0.7 reshape.81
  15.4 8.0 %fusion.8 = f32[16,4,128]{2,1,0:T(4,128)S(1)} fusion(bf16[16,4,4096]{2,1,0:T(4,128)(2,1)S(1)} %reshape.81, bf16[1,16,128,4096]{3,2,1,0:T(8,128)(2,1)} %param.5), kind=kOutput, calls=%fused_computation.8 | convolution fusion | flops 67108864 | bytes 17334272 | tf_op jit(solution)/shard_map/tsp,atrp->atsr/dot_general | solution.py:91
  23.4 0.0 copy-done.2
  23.4 0.4 fusion.7
  23.8 11.5 %all_to_all.21 = bf16[16,1,8,4,128]{4,2,3,1,0:T(8,128)(2,1)S(1)} all-to-all(bf16[16,1,8,4,128]{4,2,3,1,0:T(8,128)(2,1)S(1)} %copy.33), channel_id=1, replica_groups=mesh['ray'=16,'brick'=8] {'ray'}, dimensions={0} | all-to-all | bytes 262144 | tf_op jit(solution)/shard_map/all_to_all | solution.py:42
  35.4 10.1 %all_to_all.22 = bf16[16,1,8,4,128]{4,2,3,1,0:T(8,128)(2,1)S(1)} all-to-all(bf16[16,1,8,4,128]{4,2,3,1,0:T(8,128)(2,1)S(1)} %broadcast_in_dim.8), channel_id=1, replica_groups=mesh['ray'=16,'brick'=8] {'ray'}, dimensions={0} | all-to-all | bytes 262144 | tf_op jit(solution)/shard_map/all_to_all | solution.py:19
  45.5 0.2 convolution_convert_fusion.1
  45.7 8.0 %fusion.4 = bf16[16,4,4096]{2,1,0:T(4,128)(2,1)S(1)} fusion(bf16[1,16,128,4096]{3,2,1,0:T(8,128)(2,1)} %param.5, bf16[16,4,128]{2,0,1:T(8,128)(2,1)S(1)} %convolution_convert_fusion.1), kind=kOutput, calls=%fused_computation.4 | convolution fusion | flops 67371008 | bytes 17317888 | tf_op jit(solution)/shard_map/atsr,atrp->tsp/dot_general | solution.py:103
  53.8 0.8 convert_element_type.53
  54.6 0.7 reshape.85
  55.3 15.4 %all_to_all.23 = bf16[8,2,16384]{2,1,0:T(2,128)(2,1)S(1)} all-to-all(bf16[8,2,16384]{2,1,0:T(2,128)(2,1)S(1)} %reshape.85), channel_id=1, replica_groups=mesh['ray'=16,'brick'=8] {'brick'}, dimensions={0} | all-to-all | bytes 1048576 | tf_op jit(solution)/shard_map/all_to_all | solution.py:42
  70.6 0.7 reshape.86
  71.3 0.2 convert_reduce_fusion
  71.5 0.2 copy.40
  71.8 0.2 mul.117
  72.0 6.0 %collective-permute-start = (bf16[4,4,1,128]{3,2,1,0:T(2,128)(2,1)S(1)}, bf16[4,4,1,128]{3,2,1,0:T(2,128)(2,1)S(1)}, u32[]{:S(2)}, u32[]{:S(2)}) collective-permute-start(bf16[4,4,1,128]{3,2,1,0:T(2,128)(2,1)S(1)} %get-tuple-element.32), channel_id=1, source_target_pairs={{0,1},{1,2},{2,3},{3,4},{4,5},{5,6},{6,7},{7,8},{8,9},{9,10},{10,1... | collective-permute-start | bytes 12296 | tf_op jit(solution)/shard_map/ppermute | solution.py:54
  78.0 1.9 %collective-permute-start.1 = (bf16[4,4,1,128]{3,2,1,0:T(2,128)(2,1)S(1)}, bf16[4,4,1,128]{3,2,1,0:T(2,128)(2,1)S(1)}, u32[]{:S(2)}, u32[]{:S(2)}) collective-permute-start(bf16[4,4,1,128]{3,2,1,0:T(2,128)(2,1)S(1)} %get-tuple-element.33), channel_id=1, source_target_pairs={{1,0},{2,1},{3,2},{4,3},{5,4},{6,5},{7,6},{8,7},{9,8},{10,9},{11,1... | collective-permute-start | bytes 12296 | tf_op jit(solution)/shard_map/ppermute | solution.py:55
  80.0 0.0 collective-permute-done
  80.0 7.2 %collective-permute-done.1 = bf16[4,4,1,128]{3,2,1,0:T(2,128)(2,1)S(1)} collective-permute-done((bf16[4,4,1,128]{3,2,1,0:T(2,128)(2,1)S(1)}, bf16[4,4,1,128]{3,2,1,0:T(2,128)(2,1)S(1)}, u32[]{:S(2)}, u32[]{:S(2)}) %collective-permute-start.1) | collective-permute-done | bytes 4128 | tf_op jit(solution)/shard_map/ppermute | solution.py:55
  87.2 0.1 maximum_convert_fusion
  87.3 0.1 slice.239
  87.4 0.1 fusion.59
  87.6 0.1 fusion.60
  87.8 0.1 fusion.47
  87.9 1.9 %collective-permute-start.2 = (bf16[4,4,1,128]{3,2,1,0:T(2,128)(2,1)S(1)}, bf16[4,4,1,128]{3,2,1,0:T(2,128)(2,1)S(1)}, u32[]{:S(2)}, u32[]{:S(2)}) collective-permute-start(bf16[4,4,1,128]{3,2,1,0:T(2,128)(2,1)S(1)} %get-tuple-element.30), channel_id=1, source_target_pairs={{0,1},{1,2},{2,3},{3,4},{4,5},{5,6},{6,7},{7,8},{8,9},{9,10},{10,1... | collective-permute-start | bytes 12296 | tf_op jit(solution)/shard_map/ppermute | solution.py:54
  89.9 2.4 %collective-permute-start.3 = (bf16[4,4,1,128]{3,2,1,0:T(2,128)(2,1)S(1)}, bf16[4,4,1,128]{3,2,1,0:T(2,128)(2,1)S(1)}, u32[]{:S(2)}, u32[]{:S(2)}) collective-permute-start(bf16[4,4,1,128]{3,2,1,0:T(2,128)(2,1)S(1)} %get-tuple-element.31), channel_id=1, source_target_pairs={{1,0},{2,1},{3,2},{4,3},{5,4},{6,5},{7,6},{8,7},{9,8},{10,9},{11,1... | collective-permute-start | bytes 12296 | tf_op jit(solution)/shard_map/ppermute | solution.py:55
  92.3 6.8 %collective-permute-done.3 = bf16[4,4,1,128]{3,2,1,0:T(2,128)(2,1)S(1)} collective-permute-done((bf16[4,4,1,128]{3,2,1,0:T(2,128)(2,1)S(1)}, bf16[4,4,1,128]{3,2,1,0:T(2,128)(2,1)S(1)}, u32[]{:S(2)}, u32[]{:S(2)}) %collective-permute-start.3) | collective-permute-done | bytes 4128 | tf_op jit(solution)/shard_map/ppermute | solution.py:55
  99.1 0.1 maximum_convert_fusion.1
  99.2 0.1 slice.255
  99.3 0.1 fusion.61
  99.5 0.1 fusion.62
  99.7 0.1 fusion.48
  99.8 1.9 %collective-permute-start.4 = (bf16[4,4,1,128]{3,2,1,0:T(2,128)(2,1)S(1)}, bf16[4,4,1,128]{3,2,1,0:T(2,128)(2,1)S(1)}, u32[]{:S(2)}, u32[]{:S(2)}) collective-permute-start(bf16[4,4,1,128]{3,2,1,0:T(2,128)(2,1)S(1)} %get-tuple-element.28), channel_id=1, source_target_pairs={{0,1},{1,2},{2,3},{3,4},{4,5},{5,6},{6,7},{7,8},{8,9},{9,10},{10,1... | collective-permute-start | bytes 12296 | tf_op jit(solution)/shard_map/ppermute | solution.py:54
  101.8 2.4 %collective-permute-start.5 = (bf16[4,4,1,128]{3,2,1,0:T(2,128)(2,1)S(1)}, bf16[4,4,1,128]{3,2,1,0:T(2,128)(2,1)S(1)}, u32[]{:S(2)}, u32[]{:S(2)}) collective-permute-start(bf16[4,4,1,128]{3,2,1,0:T(2,128)(2,1)S(1)} %get-tuple-element.29), channel_id=1, source_target_pairs={{1,0},{2,1},{3,2},{4,3},{5,4},{6,5},{7,6},{8,7},{9,8},{10,9},{11,1... | collective-permute-start | bytes 12296 | tf_op jit(solution)/shard_map/ppermute | solution.py:55
  104.2 0.6 copy.41
  104.8 6.2 %collective-permute-done.5 = bf16[4,4,1,128]{3,2,1,0:T(2,128)(2,1)S(1)} collective-permute-done((bf16[4,4,1,128]{3,2,1,0:T(2,128)(2,1)S(1)}, bf16[4,4,1,128]{3,2,1,0:T(2,128)(2,1)S(1)}, u32[]{:S(2)}, u32[]{:S(2)}) %collective-permute-start.5) | collective-permute-done | bytes 4128 | tf_op jit(solution)/shard_map/ppermute | solution.py:55
  111.0 0.1 maximum_convert_fusion.2
  111.1 0.1 slice.271
  111.2 0.1 fusion.63
  111.4 0.1 fusion.64
  111.5 0.8 fusion.27
  (40 shorter events, 0.5 us)
Async XLA Ops:
  14.4 9.0 %copy-start.2 = (s32[1,16]{1,0:T(1,128)S(1)}, s32[1,16]{1,0:T(1,128)}, u32[]{:S(2)}) copy-start(s32[1,16]{1,0:T(1,128)} %param.6) | copy-start | bytes 196
  14.7 20.7 %copy-start.1 = (f32[1,8,4,128]{3,2,1,0:T(4,128)S(1)}, f32[1,8,4,128]{3,2,1,0:T(4,128)}, u32[]{:S(2)}) copy-start(f32[1,8,4,128]{3,2,1,0:T(4,128)} %param.7) | copy-start | bytes 49156
  23.4 48.5 %copy-start = (f32[4,64,128]{2,1,0:T(8,128)S(1)}, f32[4,64,128]{2,1,0:T(8,128)}, u32[]{:S(2)}) copy-start(f32[4,64,128]{2,1,0:T(8,128)} %param.4) | copy-start | bytes 393220
  72.0 7.9 %collective-permute-start = (bf16[4,4,1,128]{3,2,1,0:T(2,128)(2,1)S(1)}, bf16[4,4,1,128]{3,2,1,0:T(2,128)(2,1)S(1)}, u32[]{:S(2)}, u32[]{:S(2)}) collective-permute-start(bf16[4,4,1,128]{3,2,1,0:T(2,128)(2,1)S(1)} %get-tuple-element.32), channel_id=1, source_target_pairs={{0,1},{1,2},{2,3},{3,4},{4,5},{5,6},{6,7},{7,8},{8,9},{9,10},{10,1... | collective-permute-start | bytes 12296 | tf_op jit(solution)/shard_map/ppermute | solution.py:54
  78.0 9.2 %collective-permute-start.1 = (bf16[4,4,1,128]{3,2,1,0:T(2,128)(2,1)S(1)}, bf16[4,4,1,128]{3,2,1,0:T(2,128)(2,1)S(1)}, u32[]{:S(2)}, u32[]{:S(2)}) collective-permute-start(bf16[4,4,1,128]{3,2,1,0:T(2,128)(2,1)S(1)} %get-tuple-element.33), channel_id=1, source_target_pairs={{1,0},{2,1},{3,2},{4,3},{5,4},{6,5},{7,6},{8,7},{9,8},{10,9},{11,1... | collective-permute-start | bytes 12296 | tf_op jit(solution)/shard_map/ppermute | solution.py:55
  87.9 4.3 %collective-permute-start.2 = (bf16[4,4,1,128]{3,2,1,0:T(2,128)(2,1)S(1)}, bf16[4,4,1,128]{3,2,1,0:T(2,128)(2,1)S(1)}, u32[]{:S(2)}, u32[]{:S(2)}) collective-permute-start(bf16[4,4,1,128]{3,2,1,0:T(2,128)(2,1)S(1)} %get-tuple-element.30), channel_id=1, source_target_pairs={{0,1},{1,2},{2,3},{3,4},{4,5},{5,6},{6,7},{7,8},{8,9},{9,10},{10,1... | collective-permute-start | bytes 12296 | tf_op jit(solution)/shard_map/ppermute | solution.py:54
  89.9 9.2 %collective-permute-start.3 = (bf16[4,4,1,128]{3,2,1,0:T(2,128)(2,1)S(1)}, bf16[4,4,1,128]{3,2,1,0:T(2,128)(2,1)S(1)}, u32[]{:S(2)}, u32[]{:S(2)}) collective-permute-start(bf16[4,4,1,128]{3,2,1,0:T(2,128)(2,1)S(1)} %get-tuple-element.31), channel_id=1, source_target_pairs={{1,0},{2,1},{3,2},{4,3},{5,4},{6,5},{7,6},{8,7},{9,8},{10,9},{11,1... | collective-permute-start | bytes 12296 | tf_op jit(solution)/shard_map/ppermute | solution.py:55
  99.8 5.0 %collective-permute-start.4 = (bf16[4,4,1,128]{3,2,1,0:T(2,128)(2,1)S(1)}, bf16[4,4,1,128]{3,2,1,0:T(2,128)(2,1)S(1)}, u32[]{:S(2)}, u32[]{:S(2)}) collective-permute-start(bf16[4,4,1,128]{3,2,1,0:T(2,128)(2,1)S(1)} %get-tuple-element.28), channel_id=1, source_target_pairs={{0,1},{1,2},{2,3},{3,4},{4,5},{5,6},{6,7},{7,8},{8,9},{9,10},{10,1... | collective-permute-start | bytes 12296 | tf_op jit(solution)/shard_map/ppermute | solution.py:54
  101.8 9.2 %collective-permute-start.5 = (bf16[4,4,1,128]{3,2,1,0:T(2,128)(2,1)S(1)}, bf16[4,4,1,128]{3,2,1,0:T(2,128)(2,1)S(1)}, u32[]{:S(2)}, u32[]{:S(2)}) collective-permute-start(bf16[4,4,1,128]{3,2,1,0:T(2,128)(2,1)S(1)} %get-tuple-element.29), channel_id=1, source_target_pairs={{1,0},{2,1},{3,2},{4,3},{5,4},{6,5},{7,6},{8,7},{9,8},{10,9},{11,1... | collective-permute-start | bytes 12296 | tf_op jit(solution)/shard_map/ppermute | solution.py:55
where the time goes:
time: 113 us; the launch traced here: 112 us
  blocking collectives  49.2 us (44%)
  waiting for transfers between devices  20.2 us (18%)
  matrix products  16.7 us (15%)
  starting transfers between devices  16.5 us (15%)
  local copies, waits for them, and re-layouts  5.26 us (5%)
  other arithmetic  3.23 us (3%)
  between operations  1.15 us (1%)
    all_to_all x2, blocking collectives, sent_and_summed(): lax.all_to_all(blocks, axis, split_axis=0, concat_axis=0, tiled=True)  26.9 us
    all_to_all x2, blocking collectives, from_everyone(): lax.all_to_all(jnp.broadcast_to(array[None], (peers, *array.shape)), axis...  22.4 us
    ppermute x3, waiting for transfers between devices, padded_2(): lax.ppermute(initial, axis, [(b, a) for a, b in up])  20.2 us
    ppermute x3, starting transfers between devices, padded_2(): lax.ppermute(last, axis, up)  9.85 us
    dot_general x1, matrix products, shards(): jnp.einsum('atsr,atrp->tsp', lookup, blocks, preferred_element_type=jnp.f...  8.05 us
    dot_general x1, matrix products, shards(): jnp.einsum('tsp,atrp->atsr', tile_values, blocks, preferred_element_type=...  8.05 us
    ppermute x3, starting transfers between devices, padded_2(): lax.ppermute(initial, axis, [(b, a) for a, b in up])  6.68 us
  transfers between devices with their start and end apart: 6, of which 3 were waited for; matrix products, arithmetic and copies ran while one was open for 1% of the time, Pallas kernels for 0%

commit v1 on v0

v1 whole, which is shorter than its diff:
```python
import jax
import jax.numpy as jnp
from jax import lax
from jax.experimental import pallas as pl
from jax.experimental.pallas import tpu as pltpu
from jax.sharding import PartitionSpec as P

RAY = 16
BRICK = 8
SWEEPS = 3
MESH = pl.DeviceIdType.MESH
BF = jnp.bfloat16
F32 = jnp.float32

step_size = 0.5
tv_step = 0.28
tv_weight = 0.5


def offsets(m):
    g = m // 2
    return g + (g // 2) * (1 - 2 * (g % 2)), m % 2


def kernel(
    est_hbm, blocks_hbm, bundle_ref, sino_hbm,
    out_ref, res_ref,
    est, sino, tiles, tmp, weights, meta, contrib, picked, grad_out, grad_in,
    halo_top, halo_low, est_top, est_low, gathered, anchor,
    load_sem, weight_sem, tile_send, tile_recv, meta_send, meta_recv, con_send, con_recv,
    grad_send, grad_recv, top_send, top_recv, low_send, low_recv, edge_send, edge_recv,
):
    ray = lax.axis_index("ray")
    brick = lax.axis_index("brick")
    z, core = brick // 2, brick % 2

    def forward_peer(m):
        dz, dc = offsets(m)
        return ((z + dz) % 4) * 2 + (core + dc) % 2

    def backward_peer(m):
        dz, dc = offsets(m)
        return ((z + 4 - dz) % 4) * 2 + (core + dc) % 2

    load_est = pltpu.make_async_copy(est_hbm, est, load_sem.at[0])
    load_sino = pltpu.make_async_copy(sino_hbm, sino, load_sem.at[1])
    load_est.start()
    load_sino.start()

    def load_block(m, _):
        pltpu.make_async_copy(
            blocks_hbm.at[0, pl.ds(2 * forward_peer(m), 2)], weights.at[m], weight_sem.at[m]
        ).start()
        return 0

    lax.fori_loop(0, BRICK, load_block, 0)

    barrier = pltpu.get_barrier_semaphore()
    for m in range(1, BRICK):
        pl.semaphore_signal(
            barrier, inc=1, device_id={"ray": ray, "brick": forward_peer(m)}, device_id_type=MESH
        )
    for d in range(1, RAY):
        pl.semaphore_signal(
            barrier, inc=1, device_id={"ray": (ray + d) % RAY, "brick": brick}, device_id_type=MESH
        )

    @pl.when(brick == 0)
    def _():
        for b in range(BRICK):
            pl.semaphore_signal(
                barrier, inc=1, device_id={"ray": (ray + RAY - 1) % RAY, "brick": b}, device_id_type=MESH
            )

    @pl.when(brick == BRICK - 1)
    def _():
        for b in range(BRICK):
            pl.semaphore_signal(
                barrier, inc=1, device_id={"ray": (ray + 1) % RAY, "brick": b}, device_id_type=MESH
            )

    lane = lax.broadcasted_iota(jnp.int32, (8, 128), 1)
    row = lax.broadcasted_iota(jnp.int32, (8, 128), 0)
    lane32 = lax.broadcasted_iota(jnp.int32, (32, 128), 1)

    load_est.wait()
    for s in range(4):
        even = est[s, pl.ds(0, 32, stride=2), :]
        odd = est[s, pl.ds(1, 32, stride=2), :]
        tmp[pl.ds(s, 32, stride=8), :] = jnp.where(lane32 < 64, even, pltpu.roll(odd, 64, 1))
        tmp[pl.ds(4 + s, 32, stride=8), :] = jnp.where(lane32 < 64, pltpu.roll(even, 64, 1), odd)
    tiles[0] = tmp[...].astype(BF).reshape(16, 16, 128)

    row_keys = []
    lane_key = jnp.zeros((8, 128), F32)
    for m in range(BRICK):
        first = bundle_ref[0, 2 * forward_peer(m)].astype(F32)
        second = bundle_ref[0, 2 * forward_peer(m) + 1].astype(F32)
        both = jnp.where(row < 4, first, second)
        row_keys.append(both * 4.0 + (row % 4).astype(F32))
        lane_key = jnp.where((lane % 64) // 8 == m, jnp.where((lane // 4) % 2 == 0, first, second), lane_key)
    load_sino.wait()
    meta[0, 0:32, :] = sino[...].astype(BF)
    meta[0, 32:48, :] = jnp.concatenate([lane_key, lane_key], axis=0).astype(BF)

    pl.semaphore_wait(barrier, BRICK - 1 + RAY - 1 + 2)

    def tile_copy(m):
        return pltpu.make_async_remote_copy(
            src_ref=tiles.at[0], dst_ref=tiles.at[m], send_sem=tile_send.at[m], recv_sem=tile_recv.at[m],
            device_id={"ray": ray, "brick": backward_peer(m)}, device_id_type=MESH,
        )

    def meta_copy(d):
        return pltpu.make_async_remote_copy(
            src_ref=meta.at[0], dst_ref=meta.at[RAY - d], send_sem=meta_send.at[d], recv_sem=meta_recv.at[RAY - d],
            device_id={"ray": (ray + d) % RAY, "brick": brick}, device_id_type=MESH,
        )

    above = (brick + BRICK - 1) % BRICK
    above_ray = (ray + (brick + BRICK - 1) // BRICK + RAY - 1) % RAY
    below = (brick + 1) % BRICK
    below_ray = (ray + (brick + 1) // BRICK) % RAY
    edge_down = pltpu.make_async_remote_copy(
        src_ref=est.at[:, pl.ds(56, 8), :], dst_ref=est_top, send_sem=edge_send.at[0], recv_sem=edge_recv.at[0],
        device_id={"ray": below_ray, "brick": below}, device_id_type=MESH,
    )
    edge_up = pltpu.make_async_remote_copy(
        src_ref=est.at[:, pl.ds(0, 8), :], dst_ref=est_low, send_sem=edge_send.at[1], recv_sem=edge_recv.at[1],
        device_id={"ray": above_ray, "brick": above}, device_id_type=MESH,
    )

    for m in range(1, BRICK):
        tile_copy(m).start()
    for d in range(1, RAY):
        meta_copy(d).start()
    edge_down.start()
    edge_up.start()

    def con_copy(g, d):
        return pltpu.make_async_remote_copy(
            src_ref=contrib.at[0, pl.ds(g * 16, 16)], dst_ref=contrib.at[RAY - d, pl.ds(g * 16, 16)],
            send_sem=con_send.at[g, d], recv_sem=con_recv.at[g, RAY - d],
            device_id={"ray": (ray + d) % RAY, "brick": brick}, device_id_type=MESH,
        )

    def project(m, _):
        pltpu.make_async_copy(weights.at[m], weights.at[m], weight_sem.at[m]).wait()

        @pl.when(m > 0)
        def _():
            tile_copy(m).wait_recv()

        held = tiles[m].astype(F32)
        left = jnp.concatenate(
            [half for c in range(16) for half in (held[c, 0:8], held[c, 8:16])], axis=1
        ).astype(BF)
        full = lax.dot_general(
            left, weights[m].reshape(256, 4096), (((1,), (1,)), ((), ())), preferred_element_type=F32
        )
        picked[pl.ds(pl.multiple_of(m * 8, 8), 8), :] = jnp.where(row < 4, full[:, :128], full[:, 128:])

        @pl.when(m % 2 == 1)
        def _():
            g = m // 2
            at = pl.multiple_of(g * 16, 16)
            contrib[0, pl.ds(at, 16), :] = picked[pl.ds(at, 16), :].astype(BF)
            for d in range(1, RAY):
                con_copy(g, d).start()

        return 0

    lax.fori_loop(0, BRICK, project, 0)

    for d in range(1, RAY):
        meta_copy(d).wait_recv()
    own_first = (ray * 32).astype(F32)
    for b in range(4):
        row_keys.append(own_first + (b * 8 + row).astype(F32))
    row_keys = jnp.concatenate(row_keys, axis=0)
    columns = []
    for q in range(RAY // 2):
        key = jnp.where(
            lane < 64, meta[2 * q, 32:48, :].astype(F32)[0:8], meta[2 * q + 1, 32:48, :].astype(F32)[0:8]
        ) * 4.0 + (lane % 4).astype(F32)
        columns.append(jnp.where(row_keys == jnp.concatenate([key] * 12, axis=0), 1.0, 0.0))
    row_all = lax.broadcasted_iota(jnp.int32, (96, 128), 0)
    for q in range(4):
        owner = (ray + 4 * q + lane // 32) % RAY
        key = (owner * 32 + lane % 32).astype(F32)
        hit = (row_keys == jnp.concatenate([key] * 12, axis=0)) & (row_all < 64)
        columns.append(jnp.where(hit, -1.0, 0.0))
    select = jnp.concatenate(columns, axis=1).astype(BF)
    sinos = meta[:, 0:32, :].reshape(512, 128)

    for g in range(4):
        for d in range(1, RAY):
            con_copy(g, d).wait_recv()
    right = jnp.concatenate([contrib[...].reshape(1024, 128), sinos], axis=0)
    resid = jnp.dot(select, right, preferred_element_type=F32)
    picked[...] = resid[0:64]
    res_ref[...] = resid[64:96] - sino[...]

    def grad_copy(m):
        return pltpu.make_async_remote_copy(
            src_ref=grad_out.at[m], dst_ref=grad_in.at[m], send_sem=grad_send.at[m], recv_sem=grad_recv.at[m],
            device_id={"ray": ray, "brick": forward_peer(m)}, device_id_type=MESH,
        )

    def halo_copies(m):
        tile_row = forward_peer(m)
        down = (tile_row + 1) % BRICK
        down_ray = (ray + (tile_row + 1) // BRICK) % RAY
        up = (tile_row + BRICK - 1) % BRICK
        up_ray = (ray + (tile_row + BRICK - 1) // BRICK + RAY - 1) % RAY
        own_down = (down == brick) & (down_ray == ray)
        own_up = (up == brick) & (up_ray == ray)
        to_down = pltpu.make_async_remote_copy(
            src_ref=grad_out.at[m, 15], dst_ref=halo_top.at[brick], send_sem=top_send.at[m],
            recv_sem=top_recv.at[brick], device_id={"ray": down_ray, "brick": down}, device_id_type=MESH,
        )
        here_down = pltpu.make_async_copy(grad_out.at[m, 15], halo_top.at[brick], top_recv.at[brick])
        to_up = pltpu.make_async_remote_copy(
            src_ref=grad_out.at[m, 0], dst_ref=halo_low.at[brick], send_sem=low_send.at[m],
            recv_sem=low_recv.at[brick], device_id={"ray": up_ray, "brick": up}, device_id_type=MESH,
        )
        here_up = pltpu.make_async_copy(grad_out.at[m, 0], halo_low.at[brick], low_recv.at[brick])
        return own_down, own_up, to_down, here_down, to_up, here_up

    def backproject(step, _):
        m = BRICK - 1 - step
        mine = picked[pl.ds(pl.multiple_of(m * 8, 8), 8), :]
        left = jnp.concatenate(
            [jnp.where(row < 4, mine, 0.0), jnp.where(row < 4, 0.0, mine)], axis=1
        ).astype(BF)
        spread = jnp.dot(left, weights[m].reshape(256, 4096), preferred_element_type=F32)
        for c in range(16):
            grad_out[m, c] = jnp.concatenate(
                [spread[:, c * 256 : c * 256 + 128], spread[:, c * 256 + 128 : c * 256 + 256]], axis=0
            ).astype(BF)

        @pl.when(m > 0)
        def _():
            grad_copy(m).start()

        own_down, own_up, to_down, here_down, to_up, here_up = halo_copies(m)
        pl.when(own_down)(here_down.start)
        pl.when(jnp.logical_not(own_down))(to_down.start)
        pl.when(own_up)(here_up.start)
        pl.when(jnp.logical_not(own_up))(to_up.start)
        return 0

    lax.fori_loop(0, BRICK, backproject, 0)

    edge_down.wait_recv()
    edge_up.wait_recv()
    for b in range(BRICK):
        pltpu.make_async_copy(halo_top.at[b], halo_top.at[b], top_recv.at[b]).wait()
        pltpu.make_async_copy(halo_low.at[b], halo_low.at[b], low_recv.at[b]).wait()
    gathered[0:16, :] = halo_top[...].astype(F32).sum(axis=0)
    gathered[272:288, :] = halo_low[...].astype(F32).sum(axis=0)
    total = grad_out[0].astype(F32)
    for m in range(1, BRICK):
        grad_copy(m).wait_recv()
        total += grad_in[m].astype(F32)
    gathered[16:272, :] = total.reshape(256, 128)

    lane36 = lax.broadcasted_iota(jnp.int32, (36, 128), 1)
    for s in range(4):
        one = gathered[pl.ds(s, 36, stride=8), :]
        two = gathered[pl.ds(4 + s, 36, stride=8), :]
        anchor[s, pl.ds(0, 36, stride=2), :] = jnp.where(lane36 < 64, one, pltpu.roll(two, 64, 1))
        anchor[s, pl.ds(1, 36, stride=2), :] = jnp.where(lane36 < 64, pltpu.roll(one, 64, 1), two)
    image = jnp.concatenate([est_top[:, 4:8, :], est[...], est_low[:, 0:4, :]], axis=1)
    start = image - step_size * anchor[...]

    shape = (4, 72, 128)
    rows = lax.broadcasted_iota(jnp.int32, shape, 1)
    lanes = lax.broadcasted_iota(jnp.int32, shape, 2)
    at_start = (ray == 0) & (brick == 0)
    at_end = (ray == RAY - 1) & (brick == BRICK - 1)
    above_image = (rows < 4) & at_start
    below_image = (rows >= 68) & at_end
    last_lane = lanes == 127
    first_lane = lanes == 0
    level = jnp.zeros((1, 72, 128), F32)

    start = jnp.where(below_image, 0.0, start)
    primal = start
    extra = start
    dual_y = dual_x = dual_z = None
    for sweep in range(SWEEPS):
        diff_y = pltpu.roll(extra, 71, 1) - extra
        diff_x = jnp.where(last_lane, 0.0, pltpu.roll(extra, 127, 2)) - extra
        diff_z = jnp.concatenate([extra[1:] - extra[:-1], level], axis=0)
        trial_y, trial_x, trial_z = tv_step * diff_y, tv_step * diff_x, tv_step * diff_z
        if sweep:
            trial_y, trial_x, trial_z = dual_y + trial_y, dual_x + trial_x, dual_z + trial_z
        norm = trial_y * trial_y + trial_x * trial_x + trial_z * trial_z
        shrink = lax.rsqrt(jnp.maximum(1.0, norm * (1.0 / (tv_weight * tv_weight))))
        dual_y = jnp.where(above_image, 0.0, trial_y * shrink)
        dual_x = trial_x * shrink
        dual_z = trial_z * shrink
        div = dual_y - pltpu.roll(dual_y, 1, 1)
        div += dual_x - jnp.where(first_lane, 0.0, pltpu.roll(dual_x, 1, 2))
        div += dual_z - jnp.concatenate([level, dual_z[:-1]], axis=0)
        updated = (primal + tv_step * div + tv_step * start) * (1.0 / (1.0 + tv_step))
        extra = jnp.where(below_image, 0.0, 2.0 * updated - primal)
        primal = updated
    out_ref[...] = primal[:, 4:68, :]

    for m in range(1, BRICK):
        tile_copy(m).wait_send()
        grad_copy(m).wait_send()
    for d in range(1, RAY):
        meta_copy(d).wait_send()
        for g in range(4):
            con_copy(g, d).wait_send()
    edge_down.wait_send()
    edge_up.wait_send()
    for m in range(BRICK):
        own_down, own_up, to_down, here_down, to_up, here_up = halo_copies(m)
        pl.when(jnp.logical_not(own_down))(to_down.wait_send)
        pl.when(jnp.logical_not(own_up))(to_up.wait_send)


def shards(estimate, blocks, block_bundle, sinogram):
    dma = pltpu.SemaphoreType.DMA
    restored, residual = pl.pallas_call(
        kernel,
        out_shape=(
            jax.ShapeDtypeStruct((4, 64, 128), F32),
            jax.ShapeDtypeStruct((32, 128), F32),
        ),
        in_specs=[
            pl.BlockSpec(memory_space=pl.ANY),
            pl.BlockSpec(memory_space=pl.ANY),
            pl.BlockSpec(memory_space=pltpu.SMEM),
            pl.BlockSpec(memory_space=pl.ANY),
        ],
        out_specs=(pl.BlockSpec(memory_space=pltpu.VMEM), pl.BlockSpec(memory_space=pltpu.VMEM)),
        scratch_shapes=[
            pltpu.VMEM((4, 64, 128), F32),
            pltpu.VMEM((32, 128), F32),
            pltpu.VMEM((BRICK, 16, 16, 128), BF),
            pltpu.VMEM((256, 128), F32),
            pltpu.VMEM((BRICK, 2, 128, 4096), BF),
            pltpu.VMEM((RAY, 48, 128), BF),
            pltpu.VMEM((RAY, 64, 128), BF),
            pltpu.VMEM((64, 128), F32),
            pltpu.VMEM((BRICK, 16, 16, 128), BF),
            pltpu.VMEM((BRICK, 16, 16, 128), BF),
            pltpu.VMEM((BRICK, 16, 128), BF),
            pltpu.VMEM((BRICK, 16, 128), BF),
            pltpu.VMEM((4, 8, 128), F32),
            pltpu.VMEM((4, 8, 128), F32),
            pltpu.VMEM((288, 128), F32),
            pltpu.VMEM((4, 72, 128), F32),
            dma((2,)),
            dma((BRICK,)),
            dma((BRICK,)),
            dma((BRICK,)),
            dma((RAY,)),
            dma((RAY,)),
            dma((4, RAY)),
            dma((4, RAY)),
            dma((BRICK,)),
            dma((BRICK,)),
            dma((BRICK,)),
            dma((BRICK,)),
            dma((BRICK,)),
            dma((BRICK,)),
            dma((2,)),
            dma((2,)),
        ],
        compiler_params=pltpu.CompilerParams(
            collective_id=0, has_side_effects=True, vmem_limit_bytes=48 * 1024 * 1024
        ),
    )(estimate, blocks, block_bundle, sinogram.reshape(32, 128))
    return restored, residual.reshape(sinogram.shape)


def solution(mesh):
    return jax.shard_map(
        shards,
        mesh=mesh,
        in_specs=(
            P(None, ("ray", "brick"), None),
            P("brick", "ray", None, None),
            P("brick", "ray"),
            P("brick", "ray", None, None),
        ),
        out_specs=(P(None, ("ray", "brick"), None), P("brick", "ray", None, None)),
        check_vma=False,
    )
```

time: 113 us -> 39.7 us (0.35)
  the two profiles are of different devices: /device:TPU:121 before, /device:TPU:1 now
where the time goes in v1:
time: 39.7 us; the launch traced here: 39.5 us
  Pallas kernels  35.4 us (89%)
  local copies, waits for them, and re-layouts  3.53 us (9%)
  between operations  0.65 us (2%)
    pallas_call x1, Pallas kernels, shards(): pl.pallas_call(kernel, out_shape=(jax.ShapeDtypeStruct((4, 64, 128), F32)...  35.4 us
    unnamed x8, local copies, waits for them, and re-layouts  3.53 us

profile of v1, /device:TPU:1, one launch (start us, length us, event | category | flops | bytes accessed | tf_op | source)
XLA Modules:
  0.0 39.5 jit_solution(983699546544216242)
XLA Ops:
  0.6 0.0 copy-start
  0.6 0.9 %copy-done = f32[4,64,128]{2,1,0:T(8,128)S(1)} copy-done((f32[4,64,128]{2,1,0:T(8,128)S(1)}, f32[4,64,128]{2,1,0:T(8,128)}, u32[]{:S(2)}) %copy-start) | copy-done | bytes 131096
  1.5 0.0 copy-start.1
  1.5 0.7 %copy-done.1 = f32[1,8,4,128]{3,2,1,0:T(4,128)S(1)} copy-done((f32[1,8,4,128]{3,2,1,0:T(4,128)S(1)}, f32[1,8,4,128]{3,2,1,0:T(4,128)}, u32[]{:S(2)}) %copy-start.1) | copy-done | bytes 16408
  2.3 0.0 copy-start.2
  2.3 0.7 %copy-done.2 = s32[1,16]{1,0:T(1,128)S(1)} copy-done((s32[1,16]{1,0:T(1,128)S(1)}, s32[1,16]{1,0:T(1,128)}, u32[]{:S(2)}) %copy-start.2) | copy-done | bytes 88
  2.9 35.4 %shard_map.59 = (f32[4,64,128]{2,1,0:T(8,128)S(1)}, f32[32,128]{1,0:T(8,128)S(1)}) custom-call(f32[4,64,128]{2,1,0:T(8,128)S(1)} %copy-done, bf16[1,16,128,4096]{3,2,1,0:T(8,128)(2,1)} %blocks_hbm.1, s32[1,16]{1,0:T(1,128)S(1)} %copy-done.2, f32[32,128]{1,0:T(8,128)S(1)} %bitcast.3), custom_call_target="tpu_custom_call" | custom-call | tf_op jit(solution)/shard_map/pallas_call | solution.py:329
  38.3 0.7 %copy.8 = f32[4,64,128]{2,1,0:T(8,128)} copy(f32[4,64,128]{2,1,0:T(8,128)S(1)} %get-tuple-element.8) | data formatting | bytes 262144
  38.9 0.6 %copy.9 = f32[1,8,4,128]{3,2,1,0:T(4,128)} copy(f32[1,8,4,128]{3,2,1,0:T(4,128)S(1)} %bitcast.2) | data formatting | bytes 32768
Async XLA Ops:
  0.6 0.9 %copy-start = (f32[4,64,128]{2,1,0:T(8,128)S(1)}, f32[4,64,128]{2,1,0:T(8,128)}, u32[]{:S(2)}) copy-start(f32[4,64,128]{2,1,0:T(8,128)} %est_hbm.1) | copy-start | bytes 393220
  1.5 0.7 %copy-start.1 = (f32[1,8,4,128]{3,2,1,0:T(4,128)S(1)}, f32[1,8,4,128]{3,2,1,0:T(4,128)}, u32[]{:S(2)}) copy-start(f32[1,8,4,128]{3,2,1,0:T(4,128)} %param.7) | copy-start | bytes 49156
  2.3 0.7 %copy-start.2 = (s32[1,16]{1,0:T(1,128)S(1)}, s32[1,16]{1,0:T(1,128)}, u32[]{:S(2)}) copy-start(s32[1,16]{1,0:T(1,128)} %bundle_ref.1) | copy-start | bytes 196

commit v2 on v1

v2 whole, which is shorter than its diff:
```python
import jax
import jax.numpy as jnp
from jax import lax
from jax.experimental import pallas as pl
from jax.experimental.pallas import tpu as pltpu
from jax.sharding import PartitionSpec as P

RAY = 16
BRICK = 8
SWEEPS = 3
MESH = pl.DeviceIdType.MESH
BF = jnp.bfloat16
F32 = jnp.float32

step_size = 0.5
tv_step = 0.28
tv_weight = 0.5


def slot_offsets(m):
    third = (m + 2) // 4
    middle, last = third % 2, third // 2
    return (
        middle * (1 + 2 * (m % 2)) + 2 * last,
        middle * (m // 4) + (1 - middle) * (m % 2),
    )


def ring_step(g):
    middle = ((g + 1) // 2) % 2
    step = (2 + g + (g // 2) * (1 - 2 * (g % 2))) % 4
    return step, middle * (4 - g) + (1 - middle) * (6 - 2 * g), 1 + middle


def kernel(
    est_hbm, blocks_hbm, bundle_hbm, sino_hbm,
    out_ref, res_ref,
    bundles, est, sino, tiles, tmp, weights, meta, contrib, picked, mate_out, mate_in, grad_out, grad_in,
    halo_top, halo_low, est_edges, gathered, anchor,
    load_sem, weight_sem, tile_recv, mate_recv, send_sem, recv_sem,
):
    ray = lax.axis_index("ray")
    brick = lax.axis_index("brick")
    z, core = brick // 2, brick % 2
    mate = 2 * z + 1 - core

    def tile_row(m):
        dz, dc = slot_offsets(m)
        return ((z + dz) % 4) * 2 + (core + dc) % 2

    def remote(src, dst, send, recv, to_ray, to_brick):
        return pltpu.make_async_remote_copy(
            src_ref=src, dst_ref=dst, send_sem=send, recv_sem=recv,
            device_id={"ray": to_ray, "brick": to_brick}, device_id_type=MESH,
        )

    def wait_bytes(ref, sem):
        pltpu.make_async_copy(ref, ref, sem).wait()

    load_est = pltpu.make_async_copy(est_hbm, est, load_sem.at[0])
    load_sino = pltpu.make_async_copy(sino_hbm, sino, load_sem.at[1])
    load_bundle = pltpu.make_async_copy(bundle_hbm, bundles, load_sem.at[2])
    load_est.start()
    load_sino.start()
    load_bundle.start()

    def load_block(m, _):
        pltpu.make_async_copy(
            blocks_hbm.at[0, pl.ds(2 * tile_row(m), 2)], weights.at[m], weight_sem.at[m]
        ).start()
        return 0

    lax.fori_loop(0, BRICK, load_block, 0)

    barrier = pltpu.get_barrier_semaphore()

    def greet(to_ray, to_brick):
        pl.semaphore_signal(barrier, inc=1, device_id={"ray": to_ray, "brick": to_brick}, device_id_type=MESH)

    for m in range(1, BRICK):
        greet(ray, (brick + m) % BRICK)
    for d in range(1, RAY):
        greet((ray + d) % RAY, brick)

    @pl.when(brick == 0)
    def _():
        for b in range(4):
            greet((ray + RAY - 1) % RAY, 2 * b + 1)

    @pl.when(brick == BRICK - 1)
    def _():
        for b in range(4):
            greet((ray + 1) % RAY, 2 * b)

    lane = lax.broadcasted_iota(jnp.int32, (8, 128), 1)
    row = lax.broadcasted_iota(jnp.int32, (8, 128), 0)
    lane32 = lax.broadcasted_iota(jnp.int32, (32, 128), 1)

    load_est.wait()
    for s in range(4):
        even = est[s, pl.ds(0, 32, stride=2), :]
        odd = est[s, pl.ds(1, 32, stride=2), :]
        tmp[pl.ds(s, 32, stride=8), :] = jnp.where(lane32 < 64, even, pltpu.roll(odd, 64, 1))
        tmp[pl.ds(4 + s, 32, stride=8), :] = jnp.where(lane32 < 64, pltpu.roll(even, 64, 1), odd)
    tiles[0] = tmp[...].astype(BF).reshape(16, 16, 128)

    pl.semaphore_wait(barrier, BRICK - 1 + RAY - 1 + 1)

    remote(tiles.at[0], tiles.at[1], send_sem.at[0], tile_recv.at[1], ray, mate).start()
    for step, slot in ((1, 2), (3, 3), (2, 6)):
        to = ((z + 4 - step) % 4) * 2 + core
        remote(tiles.at[0], tiles.at[slot], send_sem.at[0], tile_recv.at[slot], ray, to).start()

    load_bundle.wait()
    row_keys = []
    lane_key = jnp.zeros((8, 128), F32)
    for m in range(BRICK):
        first = bundles[0, 2 * tile_row(m)].astype(F32)
        second = bundles[0, 2 * tile_row(m) + 1].astype(F32)
        both = jnp.where(row < 4, first, second)
        row_keys.append(both * 4.0 + (row % 4).astype(F32))
        lane_key = jnp.where((lane % 64) // 8 == m, jnp.where((lane // 4) % 2 == 0, first, second), lane_key)
    load_sino.wait()
    meta[0, 0:32, :] = sino[...].astype(BF)
    meta[0, 32:48, :] = jnp.concatenate([lane_key, lane_key], axis=0).astype(BF)
    for d in range(1, RAY):
        remote(meta.at[0], meta.at[RAY - d], send_sem.at[1], recv_sem.at[1], (ray + d) % RAY, brick).start()

    above = (brick + BRICK - 1) % BRICK
    above_ray = (ray + (brick + BRICK - 1) // BRICK + RAY - 1) % RAY
    below = (brick + 1) % BRICK
    below_ray = (ray + (brick + 1) // BRICK) % RAY
    remote(
        est.at[:, pl.ds(56, 8), :], est_edges.at[0], send_sem.at[2], recv_sem.at[2], below_ray, below
    ).start()
    remote(
        est.at[:, pl.ds(0, 8), :], est_edges.at[1], send_sem.at[2], recv_sem.at[2], above_ray, above
    ).start()

    def project(m, _):
        @pl.when(m > 0)
        def _():
            wait_bytes(tiles.at[m], tile_recv.at[m])

        @pl.when((m == 2) | (m == 3) | (m == 6))
        def _():
            slot = m + 2 - m // 6
            remote(tiles.at[m], tiles.at[slot], send_sem.at[0], tile_recv.at[slot], ray, mate).start()

        wait_bytes(weights.at[m], weight_sem.at[m])
        held = tiles[m].astype(F32)
        left = jnp.concatenate(
            [half for c in range(16) for half in (held[c, 0:8], held[c, 8:16])], axis=1
        ).astype(BF)
        full = lax.dot_general(
            left, weights[m].reshape(256, 4096), (((1,), (1,)), ((), ())), preferred_element_type=F32
        )
        picked[pl.ds(pl.multiple_of(m * 8, 8), 8), :] = jnp.where(row < 4, full[:, :128], full[:, 128:])

        @pl.when(m % 2 == 1)
        def _():
            at = pl.ds(pl.multiple_of((m // 2) * 16, 16), 16)
            contrib[0, at, :] = picked[at, :].astype(BF)
            for d in range(1, RAY):
                remote(
                    contrib.at[0, at], contrib.at[RAY - d, at], send_sem.at[3], recv_sem.at[3],
                    (ray + d) % RAY, brick,
                ).start()

        return 0

    lax.fori_loop(0, BRICK, project, 0)

    wait_bytes(meta.at[pl.ds(1, RAY - 1)], recv_sem.at[1])
    own_first = (ray * 32).astype(F32)
    for b in range(4):
        row_keys.append(own_first + (b * 8 + row).astype(F32))
    row_keys = jnp.concatenate(row_keys, axis=0)
    columns = []
    for q in range(RAY // 2):
        key = jnp.where(
            lane < 64, meta[2 * q, 32:48, :].astype(F32)[0:8], meta[2 * q + 1, 32:48, :].astype(F32)[0:8]
        ) * 4.0 + (lane % 4).astype(F32)
        columns.append(jnp.where(row_keys == jnp.concatenate([key] * 12, axis=0), 1.0, 0.0))
    row_all = lax.broadcasted_iota(jnp.int32, (96, 128), 0)
    for q in range(4):
        owner = (ray + 4 * q + lane // 32) % RAY
        key = (owner * 32 + lane % 32).astype(F32)
        hit = (row_keys == jnp.concatenate([key] * 12, axis=0)) & (row_all < 64)
        columns.append(jnp.where(hit, -1.0, 0.0))
    select = jnp.concatenate(columns, axis=1).astype(BF)
    sinos = meta[:, 0:32, :].reshape(512, 128)

    wait_bytes(contrib.at[pl.ds(1, RAY - 1)], recv_sem.at[3])
    right = jnp.concatenate([contrib[...].reshape(1024, 128), sinos], axis=0)
    resid = jnp.dot(select, right, preferred_element_type=F32)
    picked[...] = resid[0:64]
    res_ref[...] = resid[64:96] - sino[...]

    def backproject(t, _):
        pass_on = (t == 0) | ((t % 2 == 1) & (t < 7))
        g = jnp.where(pass_on, t + 1, t - 1) // 2
        dz, first, stride = ring_step(g)
        dc = jnp.where(pass_on, 1, 0)
        m = first + dc * stride
        mine = picked[pl.ds(pl.multiple_of(m * 8, 8), 8), :]
        left = jnp.concatenate(
            [jnp.where(row < 4, mine, 0.0), jnp.where(row < 4, 0.0, mine)], axis=1
        ).astype(BF)
        spread = jnp.dot(left, weights[m].reshape(256, 4096), preferred_element_type=F32)
        pieces = [
            jnp.concatenate(
                [spread[:, c * 256 : c * 256 + 128], spread[:, c * 256 + 128 : c * 256 + 256]], axis=0
            )
            for c in range(16)
        ]

        @pl.when(pass_on)
        def _():
            for c in range(16):
                mate_out[g, c] = pieces[c].astype(BF)
            remote(mate_out.at[g], mate_in.at[g], send_sem.at[4], mate_recv.at[g], ray, mate).start()

        @pl.when(jnp.logical_not(pass_on))
        def _():
            wait_bytes(mate_in.at[g], mate_recv.at[g])
            for c in range(16):
                grad_out[g, c] = (pieces[c] + mate_in[g, c].astype(F32)).astype(BF)
            target = ((z + dz) % 4) * 2 + core

            @pl.when(g < 3)
            def _():
                remote(grad_out.at[g], grad_in.at[g], send_sem.at[5], recv_sem.at[5], ray, target).start()

            remote(
                grad_out.at[g, 15], halo_top.at[z], send_sem.at[6], recv_sem.at[6],
                (ray + (target + 1) // BRICK) % RAY, (target + 1) % BRICK,
            ).start()
            remote(
                grad_out.at[g, 0], halo_low.at[z], send_sem.at[7], recv_sem.at[7],
                (ray + (target + BRICK - 1) // BRICK + RAY - 1) % RAY, (target + BRICK - 1) % BRICK,
            ).start()

        return 0

    lax.fori_loop(0, BRICK, backproject, 0)

    wait_bytes(est_edges, recv_sem.at[2])
    wait_bytes(grad_in, recv_sem.at[5])
    total = grad_out[3].astype(F32)
    for g in range(3):
        total += grad_in[g].astype(F32)
    gathered[16:272, :] = total.reshape(256, 128)
    wait_bytes(halo_top, recv_sem.at[6])
    wait_bytes(halo_low, recv_sem.at[7])
    gathered[0:16, :] = halo_top[...].astype(F32).sum(axis=0)
    gathered[272:288, :] = halo_low[...].astype(F32).sum(axis=0)

    lane36 = lax.broadcasted_iota(jnp.int32, (36, 128), 1)
    for s in range(4):
        one = gathered[pl.ds(s, 36, stride=8), :]
        two = gathered[pl.ds(4 + s, 36, stride=8), :]
        anchor[s, pl.ds(0, 36, stride=2), :] = jnp.where(lane36 < 64, one, pltpu.roll(two, 64, 1))
        anchor[s, pl.ds(1, 36, stride=2), :] = jnp.where(lane36 < 64, pltpu.roll(one, 64, 1), two)
    image = jnp.concatenate([est_edges[0, :, 4:8, :], est[...], est_edges[1, :, 0:4, :]], axis=1)
    start = image - step_size * anchor[...]

    shape = (4, 72, 128)
    rows = lax.broadcasted_iota(jnp.int32, shape, 1)
    lanes = lax.broadcasted_iota(jnp.int32, shape, 2)
    at_start = (ray == 0) & (brick == 0)
    at_end = (ray == RAY - 1) & (brick == BRICK - 1)
    above_image = (rows < 4) & at_start
    below_image = (rows >= 68) & at_end
    last_lane = lanes == 127
    first_lane = lanes == 0
    level = jnp.zeros((1, 72, 128), F32)

    start = jnp.where(below_image, 0.0, start)
    primal = start
    extra = start
    dual_y = dual_x = dual_z = None
    for sweep in range(SWEEPS):
        diff_y = pltpu.roll(extra, 71, 1) - extra
        diff_x = jnp.where(last_lane, 0.0, pltpu.roll(extra, 127, 2)) - extra
        diff_z = jnp.concatenate([extra[1:] - extra[:-1], level], axis=0)
        trial_y, trial_x, trial_z = tv_step * diff_y, tv_step * diff_x, tv_step * diff_z
        if sweep:
            trial_y, trial_x, trial_z = dual_y + trial_y, dual_x + trial_x, dual_z + trial_z
        norm = trial_y * trial_y + trial_x * trial_x + trial_z * trial_z
        shrink = lax.rsqrt(jnp.maximum(1.0, norm * (1.0 / (tv_weight * tv_weight))))
        dual_y = jnp.where(above_image, 0.0, trial_y * shrink)
        dual_x = trial_x * shrink
        dual_z = trial_z * shrink
        div = dual_y - pltpu.roll(dual_y, 1, 1)
        div += dual_x - jnp.where(first_lane, 0.0, pltpu.roll(dual_x, 1, 2))
        div += dual_z - jnp.concatenate([level, dual_z[:-1]], axis=0)
        updated = (primal + tv_step * div + tv_step * start) * (1.0 / (1.0 + tv_step))
        extra = jnp.where(below_image, 0.0, 2.0 * updated - primal)
        primal = updated
    out_ref[...] = primal[:, 4:68, :]

    wait_bytes(tiles.at[pl.ds(1, BRICK - 1)], send_sem.at[0])
    wait_bytes(meta.at[pl.ds(1, RAY - 1)], send_sem.at[1])
    wait_bytes(est_edges, send_sem.at[2])
    wait_bytes(contrib.at[pl.ds(1, RAY - 1)], send_sem.at[3])
    wait_bytes(mate_in, send_sem.at[4])
    wait_bytes(grad_in, send_sem.at[5])
    wait_bytes(halo_top, send_sem.at[6])
    wait_bytes(halo_low, send_sem.at[7])


def shards(estimate, blocks, block_bundle, sinogram):
    dma = pltpu.SemaphoreType.DMA
    inputs = (estimate, blocks, block_bundle, sinogram.reshape(32, 128))
    restored, residual = pl.pallas_call(
        kernel,
        out_shape=(
            jax.ShapeDtypeStruct((4, 64, 128), F32),
            jax.ShapeDtypeStruct((32, 128), F32),
        ),
        in_specs=[pl.BlockSpec(memory_space=pltpu.HBM)] * 4,
        out_specs=(pl.BlockSpec(memory_space=pltpu.VMEM), pl.BlockSpec(memory_space=pltpu.VMEM)),
        scratch_shapes=[
            pltpu.SMEM((1, 16), jnp.int32),
            pltpu.VMEM((4, 64, 128), F32),
            pltpu.VMEM((32, 128), F32),
            pltpu.VMEM((BRICK, 16, 16, 128), BF),
            pltpu.VMEM((256, 128), F32),
            pltpu.VMEM((BRICK, 2, 128, 4096), BF),
            pltpu.VMEM((RAY, 48, 128), BF),
            pltpu.VMEM((RAY, 64, 128), BF),
            pltpu.VMEM((64, 128), F32),
            pltpu.VMEM((4, 16, 16, 128), BF),
            pltpu.VMEM((4, 16, 16, 128), BF),
            pltpu.VMEM((4, 16, 16, 128), BF),
            pltpu.VMEM((3, 16, 16, 128), BF),
            pltpu.VMEM((4, 16, 128), BF),
            pltpu.VMEM((4, 16, 128), BF),
            pltpu.VMEM((2, 4, 8, 128), F32),
            pltpu.VMEM((288, 128), F32),
            pltpu.VMEM((4, 72, 128), F32),
            dma((3,)),
            dma((BRICK,)),
            dma((BRICK,)),
            dma((4,)),
            dma((8,)),
            dma((8,)),
        ],
        compiler_params=pltpu.CompilerParams(
            collective_id=0, has_side_effects=True, vmem_limit_bytes=48 * 1024 * 1024
        ),
    )(*(pltpu.with_memory_space_constraint(array, pltpu.HBM) for array in inputs))
    return restored, residual.reshape(sinogram.shape)


def solution(mesh):
    return jax.shard_map(
        shards,
        mesh=mesh,
        in_specs=(
            P(None, ("ray", "brick"), None),
            P("brick", "ray", None, None),
            P("brick", "ray"),
            P("brick", "ray", None, None),
        ),
        out_specs=(P(None, ("ray", "brick"), None), P("brick", "ray", None, None)),
        check_vma=False,
    )
```

time: 39.7 us -> 33.1 us (0.83)
  the two profiles are of different devices: /device:TPU:1 before, /device:TPU:0 now
where the time goes in v2:
time: 33.1 us; the launch traced here: 33 us
  Pallas kernels  31.1 us (94%)
  local copies, waits for them, and re-layouts  1.26 us (4%)
  between operations  0.64 us (2%)
    pallas_call x1, Pallas kernels, shards(): pl.pallas_call(kernel, out_shape=(jax.ShapeDtypeStruct((4, 64, 128), F32)...  31.1 us
    unnamed x2, local copies, waits for them, and re-layouts  1.26 us

profile of v2, /device:TPU:0, one launch (start us, length us, event | category | flops | bytes accessed | tf_op | source)
XLA Modules:
  0.0 33.0 jit_solution(17475056308116511432)
XLA Ops:
  0.6 31.1 %shard_map.59 = (f32[4,64,128]{2,1,0:T(8,128)S(1)}, f32[32,128]{1,0:T(8,128)S(1)}) custom-call(f32[4,64,128]{2,1,0:T(8,128)} %est_hbm.1, bf16[1,16,128,4096]{3,2,1,0:T(8,128)(2,1)} %blocks_hbm.1, s32[1,16]{1,0:T(1,128)} %bundle_hbm.1, f32[32,128]{1,0:T(8,128)} %bitcast.3), custom_call_target="tpu_custom_call" | custom-call | tf_op jit(solution)/shard_map/pallas_call | solution.py:316
  31.7 0.7 %copy.8 = f32[4,64,128]{2,1,0:T(8,128)} copy(f32[4,64,128]{2,1,0:T(8,128)S(1)} %get-tuple-element.8) | data formatting | bytes 262144
  32.4 0.6 %copy.9 = f32[1,8,4,128]{3,2,1,0:T(4,128)} copy(f32[1,8,4,128]{3,2,1,0:T(4,128)S(1)} %bitcast.2) | data formatting | bytes 32768

commit v3 on v2

--- a/solution.py
+++ b/solution.py
@@ -24,6 +24,12 @@
         middle * (1 + 2 * (m % 2)) + 2 * last,
         middle * (m // 4) + (1 - middle) * (m % 2),
     )
+
+
+RAY_STEPS = sorted(
+    ((dx, dy) for dx in range(4) for dy in range(4) if dx or dy),
+    key=lambda step: -(min(step[0], 4 - step[0]) + min(step[1], 4 - step[1])),
+)
 
 
 def ring_step(g):
@@ -43,6 +49,13 @@
     brick = lax.axis_index("brick")
     z, core = brick // 2, brick % 2
     mate = 2 * z + 1 - core
+    ray_x, ray_y = ray // 4, ray % 4
+
+    def ray_peer(dx, dy):
+        return ((ray_x + dx) % 4) * 4 + (ray_y + dy) % 4
+
+    def ray_slot(dx, dy):
+        return ((4 - dx) % 4) * 4 + (4 - dy) % 4
 
     def tile_row(m):
         dz, dc = slot_offsets(m)
@@ -61,6 +74,27 @@
     load_sino = pltpu.make_async_copy(sino_hbm, sino, load_sem.at[1])
     load_bundle = pltpu.make_async_copy(bundle_hbm, bundles, load_sem.at[2])
     load_est.start()
+
+    barrier = pltpu.get_barrier_semaphore()
+
+    def greet(to_ray, to_brick):
+        pl.semaphore_signal(barrier, inc=1, device_id={"ray": to_ray, "brick": to_brick}, device_id_type=MESH)
+
+    for m in range(1, BRICK):
+        greet(ray, (brick + m) % BRICK)
+    for dx, dy in RAY_STEPS:
+        greet(ray_peer(dx, dy), brick)
+
+    @pl.when(brick == 0)
+    def _():
+        for b in range(4):
+            greet((ray + RAY - 1) % RAY, 2 * b + 1)
+
+    @pl.when(brick == BRICK - 1)
+    def _():
+        for b in range(4):
+            greet((ray + 1) % RAY, 2 * b)
+
     load_sino.start()
     load_bundle.start()
 
@@ -71,26 +105,6 @@
         return 0
 
     lax.fori_loop(0, BRICK, load_block, 0)
-
-    barrier = pltpu.get_barrier_semaphore()
-
-    def greet(to_ray, to_brick):
-        pl.semaphore_signal(barrier, inc=1, device_id={"ray": to_ray, "brick": to_brick}, device_id_type=MESH)
-
-    for m in range(1, BRICK):
-        greet(ray, (brick + m) % BRICK)
-    for d in range(1, RAY):
-        greet((ray + d) % RAY, brick)
-
-    @pl.when(brick == 0)
-    def _():
-        for b in range(4):
-            greet((ray + RAY - 1) % RAY, 2 * b + 1)
-
-    @pl.when(brick == BRICK - 1)
-    def _():
-        for b in range(4):
-            greet((ray + 1) % RAY, 2 * b)
 
     lane = lax.broadcasted_iota(jnp.int32, (8, 128), 1)
     row = lax.broadcasted_iota(jnp.int32, (8, 128), 0)
@@ -123,8 +137,10 @@
     load_sino.wait()
     meta[0, 0:32, :] = sino[...].astype(BF)
     meta[0, 32:48, :] = jnp.concatenate([lane_key, lane_key], axis=0).astype(BF)
-    for d in range(1, RAY):
-        remote(meta.at[0], meta.at[RAY - d], send_sem.at[1], recv_sem.at[1], (ray + d) % RAY, brick).start()
+    for dx, dy in RAY_STEPS:
+        remote(
+            meta.at[0], meta.at[ray_slot(dx, dy)], send_sem.at[1], recv_sem.at[1], ray_peer(dx, dy), brick
+        ).start()
 
     above = (brick + BRICK - 1) % BRICK
     above_ray = (ray + (brick + BRICK - 1) // BRICK + RAY - 1) % RAY
@@ -157,16 +173,16 @@
         )
         picked[pl.ds(pl.multiple_of(m * 8, 8), 8), :] = jnp.where(row < 4, full[:, :128], full[:, 128:])
 
-        @pl.when(m % 2 == 1)
-        def _():
-            at = pl.ds(pl.multiple_of((m // 2) * 16, 16), 16)
+        def hand_out(at):
             contrib[0, at, :] = picked[at, :].astype(BF)
-            for d in range(1, RAY):
+            for dx, dy in RAY_STEPS:
                 remote(
-                    contrib.at[0, at], contrib.at[RAY - d, at], send_sem.at[3], recv_sem.at[3],
-                    (ray + d) % RAY, brick,
+                    contrib.at[0, at], contrib.at[ray_slot(dx, dy), at], send_sem.at[3], recv_sem.at[3],
+                    ray_peer(dx, dy), brick,
                 ).start()
 
+        pl.when(m == 5)(lambda: hand_out(pl.ds(0, 48)))
+        pl.when(m == 7)(lambda: hand_out(pl.ds(48, 16)))
         return 0
 
     lax.fori_loop(0, BRICK, project, 0)
@@ -184,7 +200,7 @@
         columns.append(jnp.where(row_keys == jnp.concatenate([key] * 12, axis=0), 1.0, 0.0))
     row_all = lax.broadcasted_iota(jnp.int32, (96, 128), 0)
     for q in range(4):
-        owner = (ray + 4 * q + lane // 32) % RAY
+        owner = ((ray_x + q) % 4) * 4 + (ray_y + lane // 32) % 4
         key = (owner * 32 + lane % 32).astype(F32)
         hit = (row_keys == jnp.concatenate([key] * 12, axis=0)) & (row_all < 64)
         columns.append(jnp.where(hit, -1.0, 0.0))
@@ -265,6 +281,25 @@
     image = jnp.concatenate([est_edges[0, :, 4:8, :], est[...], est_edges[1, :, 0:4, :]], axis=1)
     start = image - step_size * anchor[...]
 
+    out_ref[...] = start
+
+    wait_bytes(tiles.at[pl.ds(1, BRICK - 1)], send_sem.at[0])
+    wait_bytes(meta.at[pl.ds(1, RAY - 1)], send_sem.at[1])
+    wait_bytes(est_edges, send_sem.at[2])
+    wait_bytes(contrib.at[pl.ds(1, RAY - 1)], send_sem.at[3])
+    wait_bytes(mate_in, send_sem.at[4])
+    wait_bytes(grad_in, send_sem.at[5])
+    wait_bytes(halo_top, send_sem.at[6])
+    wait_bytes(halo_low, send_sem.at[7])
+
+
+def sweeps_kernel(start_ref, res_ref, out_hbm, res_hbm, out, save_sem):
+    ray = lax.axis_index("ray")
+    brick = lax.axis_index("brick")
+    save_res = pltpu.make_async_copy(res_ref, res_hbm, save_sem.at[0])
+    save_out = pltpu.make_async_copy(out, out_hbm, save_sem.at[1])
+    save_res.start()
+
     shape = (4, 72, 128)
     rows = lax.broadcasted_iota(jnp.int32, shape, 1)
     lanes = lax.broadcasted_iota(jnp.int32, shape, 2)
@@ -276,7 +311,7 @@
     first_lane = lanes == 0
     level = jnp.zeros((1, 72, 128), F32)
 
-    start = jnp.where(below_image, 0.0, start)
+    start = jnp.where(below_image, 0.0, start_ref[...])
     primal = start
     extra = start
     dual_y = dual_x = dual_z = None
@@ -298,25 +333,19 @@
         updated = (primal + tv_step * div + tv_step * start) * (1.0 / (1.0 + tv_step))
         extra = jnp.where(below_image, 0.0, 2.0 * updated - primal)
         primal = updated
-    out_ref[...] = primal[:, 4:68, :]
-
-    wait_bytes(tiles.at[pl.ds(1, BRICK - 1)], send_sem.at[0])
-    wait_bytes(meta.at[pl.ds(1, RAY - 1)], send_sem.at[1])
-    wait_bytes(est_edges, send_sem.at[2])
-    wait_bytes(contrib.at[pl.ds(1, RAY - 1)], send_sem.at[3])
-    wait_bytes(mate_in, send_sem.at[4])
-    wait_bytes(grad_in, send_sem.at[5])
-    wait_bytes(halo_top, send_sem.at[6])
-    wait_bytes(halo_low, send_sem.at[7])
+    out[...] = primal[:, 4:68, :]
+    save_out.start()
+    save_res.wait()
+    save_out.wait()
 
 
 def shards(estimate, blocks, block_bundle, sinogram):
     dma = pltpu.SemaphoreType.DMA
     inputs = (estimate, blocks, block_bundle, sinogram.reshape(32, 128))
-    restored, residual = pl.pallas_call(
+    start, residual = pl.pallas_call(
         kernel,
         out_shape=(
-            jax.ShapeDtypeStruct((4, 64, 128), F32),
+            jax.ShapeDtypeStruct((4, 72, 128), F32),
             jax.ShapeDtypeStruct((32, 128), F32),
         ),
         in_specs=[pl.BlockSpec(memory_space=pltpu.HBM)] * 4,
@@ -351,6 +380,17 @@
             collective_id=0, has_side_effects=True, vmem_limit_bytes=48 * 1024 * 1024
         ),
     )(*(pltpu.with_memory_space_constraint(array, pltpu.HBM) for array in inputs))
+    restored, residual = pl.pallas_call(
+        sweeps_kernel,
+        out_shape=(
+            jax.ShapeDtypeStruct((4, 64, 128), F32),
+            jax.ShapeDtypeStruct((32, 128), F32),
+        ),
+        in_specs=[pl.BlockSpec(memory_space=pltpu.VMEM)] * 2,
+        out_specs=(pl.BlockSpec(memory_space=pltpu.HBM),) * 2,
+        scratch_shapes=[pltpu.VMEM((4, 64, 128), F32), dma((2,))],
+        compiler_params=pltpu.CompilerParams(vmem_limit_bytes=16 * 1024 * 1024),
+    )(start, residual)
     return restored, residual.reshape(sinogram.shape)
 
 

time: 33.1 us -> 32.4 us (0.979)
  local copies, waits for them, and re-layouts: 1.26 us -> 0 us
  Pallas kernels: 31.1 us -> 31.6 us
    unnamed x2 -> x0, local copies, waits for them, and re-layouts: 1.26 us -> none
    pallas_call x1 -> x2, Pallas kernels: 31.1 us -> 31.6 us  [the longest x1 30.3 us: shards(): pl.pallas_call(kernel, out_shape=(jax.ShapeDtypeStruct((4, 72, 128), F32)...]
where the time goes in v3:
time: 32.4 us; the launch traced here: 32.2 us
  Pallas kernels  31.6 us (98%)
  between operations  0.64 us (2%)
    pallas_call x1, Pallas kernels, shards(): pl.pallas_call(kernel, out_shape=(jax.ShapeDtypeStruct((4, 72, 128), F32)...  30.3 us
    pallas_call x1, Pallas kernels, shards(): pl.pallas_call(sweeps_kernel, out_shape=(jax.ShapeDtypeStruct((4, 64, 128...  1.32 us

profile of v3, /device:TPU:0, one launch (start us, length us, event | category | flops | bytes accessed | tf_op | source)
XLA Modules:
  0.0 32.2 jit_solution(1682141967055359276)
XLA Ops:
  0.6 30.3 %shard_map.59 = (f32[4,72,128]{2,1,0:T(8,128)S(1)}, f32[32,128]{1,0:T(8,128)S(1)}) custom-call(f32[4,64,128]{2,1,0:T(8,128)} %est_hbm.1, bf16[1,16,128,4096]{3,2,1,0:T(8,128)(2,1)} %blocks_hbm.1, s32[1,16]{1,0:T(1,128)} %bundle_hbm.1, f32[32,128]{1,0:T(8,128)} %bitcast.2), custom_call_target="tpu_custom_call" | custom-call | tf_op jit(solution)/shard_map/pallas_call | solution.py:345
  30.9 1.3 %shard_map.60 = (f32[4,64,128]{2,1,0:T(8,128)}, f32[32,128]{1,0:T(8,128)}) custom-call(f32[4,72,128]{2,1,0:T(8,128)S(1)} %get-tuple-element.6.start_ref, f32[32,128]{1,0:T(8,128)S(1)} %get-tuple-element.7.res_ref), custom_call_target="tpu_custom_call" | custom-call | tf_op jit(solution)/shard_map/pallas_call | solution.py:383

commit v4 on v3

--- a/solution.py
+++ b/solution.py
@@ -42,7 +42,7 @@
     est_hbm, blocks_hbm, bundle_hbm, sino_hbm,
     out_ref, res_ref,
     bundles, est, sino, tiles, tmp, weights, meta, contrib, picked, mate_out, mate_in, grad_out, grad_in,
-    halo_top, halo_low, est_edges, gathered, anchor,
+    halo_top, halo_low, far_out, far_in, est_edges, gathered, anchor,
     load_sem, weight_sem, tile_recv, mate_recv, send_sem, recv_sem,
 ):
     ray = lax.axis_index("ray")
@@ -87,13 +87,13 @@
 
     @pl.when(brick == 0)
     def _():
-        for b in range(4):
-            greet((ray + RAY - 1) % RAY, 2 * b + 1)
+        for b in range(BRICK):
+            greet((ray + RAY - 1) % RAY, b)
 
     @pl.when(brick == BRICK - 1)
     def _():
-        for b in range(4):
-            greet((ray + 1) % RAY, 2 * b)
+        for b in range(BRICK):
+            greet((ray + 1) % RAY, b)
 
     load_sino.start()
     load_bundle.start()
@@ -118,7 +118,7 @@
         tmp[pl.ds(4 + s, 32, stride=8), :] = jnp.where(lane32 < 64, pltpu.roll(even, 64, 1), odd)
     tiles[0] = tmp[...].astype(BF).reshape(16, 16, 128)
 
-    pl.semaphore_wait(barrier, BRICK - 1 + RAY - 1 + 1)
+    pl.semaphore_wait(barrier, BRICK - 1 + RAY - 1 + 2)
 
     remote(tiles.at[0], tiles.at[1], send_sem.at[0], tile_recv.at[1], ray, mate).start()
     for step, slot in ((1, 2), (3, 3), (2, 6)):
@@ -213,17 +213,35 @@
     picked[...] = resid[0:64]
     res_ref[...] = resid[64:96] - sino[...]
 
+    def split_left(m):
+        mine = picked[pl.ds(pl.multiple_of(m * 8, 8), 8), :]
+        return jnp.concatenate(
+            [jnp.where(row < 4, mine, 0.0), jnp.where(row < 4, 0.0, mine)], axis=1
+        ).astype(BF)
+
+    for edge, (last, column) in enumerate(((BRICK - 1, 15), (0, 0))):
+        dz = (last // 2 + 4 - z) % 4
+        dc = (last + core) % 2
+        odd = dz % 2
+        m = odd * (2 + dz // 2 + 2 * dc) + (1 - odd) * (3 * dz + dc)
+        rim = jnp.dot(
+            split_left(m),
+            weights[m, :, :, column * 256 : column * 256 + 256].reshape(256, 256),
+            preferred_element_type=F32,
+        )
+        far_out[edge] = jnp.concatenate([rim[:, :128], rim[:, 128:]], axis=0).astype(BF)
+        remote(
+            far_out.at[edge], far_in.at[brick], send_sem.at[7], recv_sem.at[7],
+            (ray + (1, RAY - 1)[edge]) % RAY, (0, BRICK - 1)[edge],
+        ).start()
+
     def backproject(t, _):
         pass_on = (t == 0) | ((t % 2 == 1) & (t < 7))
         g = jnp.where(pass_on, t + 1, t - 1) // 2
         dz, first, stride = ring_step(g)
         dc = jnp.where(pass_on, 1, 0)
         m = first + dc * stride
-        mine = picked[pl.ds(pl.multiple_of(m * 8, 8), 8), :]
-        left = jnp.concatenate(
-            [jnp.where(row < 4, mine, 0.0), jnp.where(row < 4, 0.0, mine)], axis=1
-        ).astype(BF)
-        spread = jnp.dot(left, weights[m].reshape(256, 4096), preferred_element_type=F32)
+        spread = jnp.dot(split_left(m), weights[m].reshape(256, 4096), preferred_element_type=F32)
         pieces = [
             jnp.concatenate(
                 [spread[:, c * 256 : c * 256 + 128], spread[:, c * 256 + 128 : c * 256 + 256]], axis=0
@@ -248,14 +266,17 @@
             def _():
                 remote(grad_out.at[g], grad_in.at[g], send_sem.at[5], recv_sem.at[5], ray, target).start()
 
-            remote(
-                grad_out.at[g, 15], halo_top.at[z], send_sem.at[6], recv_sem.at[6],
-                (ray + (target + 1) // BRICK) % RAY, (target + 1) % BRICK,
-            ).start()
-            remote(
-                grad_out.at[g, 0], halo_low.at[z], send_sem.at[7], recv_sem.at[7],
-                (ray + (target + BRICK - 1) // BRICK + RAY - 1) % RAY, (target + BRICK - 1) % BRICK,
-            ).start()
+            @pl.when(target < BRICK - 1)
+            def _():
+                remote(
+                    grad_out.at[g, 15], halo_top.at[z], send_sem.at[6], recv_sem.at[6], ray, target + 1
+                ).start()
+
+            @pl.when(target > 0)
+            def _():
+                remote(
+                    grad_out.at[g, 0], halo_low.at[z], send_sem.at[6], recv_sem.at[8], ray, target - 1
+                ).start()
 
         return 0
 
@@ -267,10 +288,26 @@
     for g in range(3):
         total += grad_in[g].astype(F32)
     gathered[16:272, :] = total.reshape(256, 128)
-    wait_bytes(halo_top, recv_sem.at[6])
-    wait_bytes(halo_low, recv_sem.at[7])
-    gathered[0:16, :] = halo_top[...].astype(F32).sum(axis=0)
-    gathered[272:288, :] = halo_low[...].astype(F32).sum(axis=0)
+
+    @pl.when(brick > 0)
+    def _():
+        wait_bytes(halo_top, recv_sem.at[6])
+        gathered[0:16, :] = halo_top[...].astype(F32).sum(axis=0)
+
+    @pl.when(brick < BRICK - 1)
+    def _():
+        wait_bytes(halo_low, recv_sem.at[8])
+        gathered[272:288, :] = halo_low[...].astype(F32).sum(axis=0)
+
+    @pl.when(brick == 0)
+    def _():
+        wait_bytes(far_in, recv_sem.at[7])
+        gathered[0:16, :] = far_in[...].astype(F32).sum(axis=0)
+
+    @pl.when(brick == BRICK - 1)
+    def _():
+        wait_bytes(far_in, recv_sem.at[7])
+        gathered[272:288, :] = far_in[...].astype(F32).sum(axis=0)
 
     lane36 = lax.broadcasted_iota(jnp.int32, (36, 128), 1)
     for s in range(4):
@@ -289,8 +326,8 @@
     wait_bytes(contrib.at[pl.ds(1, RAY - 1)], send_sem.at[3])
     wait_bytes(mate_in, send_sem.at[4])
     wait_bytes(grad_in, send_sem.at[5])
-    wait_bytes(halo_top, send_sem.at[6])
-    wait_bytes(halo_low, send_sem.at[7])
+    wait_bytes(tiles.at[0, pl.ds(0, 7)], send_sem.at[6])
+    wait_bytes(far_out, send_sem.at[7])
 
 
 def sweeps_kernel(start_ref, res_ref, out_hbm, res_hbm, out, save_sem):
@@ -366,6 +403,8 @@
             pltpu.VMEM((3, 16, 16, 128), BF),
             pltpu.VMEM((4, 16, 128), BF),
             pltpu.VMEM((4, 16, 128), BF),
+            pltpu.VMEM((2, 16, 128), BF),
+            pltpu.VMEM((BRICK, 16, 128), BF),
             pltpu.VMEM((2, 4, 8, 128), F32),
             pltpu.VMEM((288, 128), F32),
             pltpu.VMEM((4, 72, 128), F32),
@@ -374,7 +413,7 @@
             dma((BRICK,)),
             dma((4,)),
             dma((8,)),
-            dma((8,)),
+            dma((9,)),
         ],
         compiler_params=pltpu.CompilerParams(
             collective_id=0, has_side_effects=True, vmem_limit_bytes=48 * 1024 * 1024

time: 32.4 us -> 31.6 us (0.975)
  the two profiles are of different devices: /device:TPU:0 before, /device:TPU:1 now
where the time goes in v4:
time: 31.6 us; the launch traced here: 31.4 us
  Pallas kernels  30.8 us (97%)
  between operations  0.64 us (2%)
    pallas_call x1, Pallas kernels, shards(): pl.pallas_call(kernel, out_shape=(jax.ShapeDtypeStruct((4, 72, 128), F32)...  29.5 us
    pallas_call x1, Pallas kernels, shards(): pl.pallas_call(sweeps_kernel, out_shape=(jax.ShapeDtypeStruct((4, 64, 128...  1.32 us

profile of v4, /device:TPU:1, one launch (start us, length us, event | category | flops | bytes accessed | tf_op | source)
XLA Modules:
  0.0 31.4 jit_solution(9376336563631833573)
XLA Ops:
  0.6 29.5 %shard_map.59 = (f32[4,72,128]{2,1,0:T(8,128)S(1)}, f32[32,128]{1,0:T(8,128)S(1)}) custom-call(f32[4,64,128]{2,1,0:T(8,128)} %est_hbm.1, bf16[1,16,128,4096]{3,2,1,0:T(8,128)(2,1)} %blocks_hbm.1, s32[1,16]{1,0:T(1,128)} %bundle_hbm.1, f32[32,128]{1,0:T(8,128)} %bitcast.2), custom_call_target="tpu_custom_call" | custom-call | tf_op jit(solution)/shard_map/pallas_call | solution.py:382
  30.1 1.3 %shard_map.60 = (f32[4,64,128]{2,1,0:T(8,128)}, f32[32,128]{1,0:T(8,128)}) custom-call(f32[4,72,128]{2,1,0:T(8,128)S(1)} %get-tuple-element.6.start_ref, f32[32,128]{1,0:T(8,128)S(1)} %get-tuple-element.7.res_ref), custom_call_target="tpu_custom_call" | custom-call | tf_op jit(solution)/shard_map/pallas_call | solution.py:422

commit v5 on v4

--- a/solution.py
+++ b/solution.py
@@ -26,22 +26,19 @@
     )
 
 
-RAY_STEPS = sorted(
-    ((dx, dy) for dx in range(4) for dy in range(4) if dx or dy),
-    key=lambda step: -(min(step[0], 4 - step[0]) + min(step[1], 4 - step[1])),
-)
+def far_first(g):
+    return (2 + g + (g // 2) * (1 - 2 * (g % 2))) % 4
 
 
 def ring_step(g):
     middle = ((g + 1) // 2) % 2
-    step = (2 + g + (g // 2) * (1 - 2 * (g % 2))) % 4
-    return step, middle * (4 - g) + (1 - middle) * (6 - 2 * g), 1 + middle
+    return far_first(g), middle * (4 - g) + (1 - middle) * (6 - 2 * g), 1 + middle
 
 
 def kernel(
     est_hbm, blocks_hbm, bundle_hbm, sino_hbm,
     out_ref, res_ref,
-    bundles, est, sino, tiles, tmp, weights, meta, contrib, picked, mate_out, mate_in, grad_out, grad_in,
+    bundles, est, sino, tiles, tmp, weights, meta, contrib, picked, select_own, stage, mate_out, mate_in, grad_out, grad_in,
     halo_top, halo_low, far_out, far_in, est_edges, gathered, anchor,
     load_sem, weight_sem, tile_recv, mate_recv, send_sem, recv_sem,
 ):
@@ -51,11 +48,17 @@
     mate = 2 * z + 1 - core
     ray_x, ray_y = ray // 4, ray % 4
 
-    def ray_peer(dx, dy):
-        return ((ray_x + dx) % 4) * 4 + (ray_y + dy) % 4
-
-    def ray_slot(dx, dy):
-        return ((4 - dx) % 4) * 4 + (4 - dy) % 4
+    def each(count, body):
+        def step(n, _):
+            body(n)
+            return 0
+
+        lax.fori_loop(0, count, step, 0)
+
+    def ray_step(n):
+        dx, dy = far_first(n // 4), far_first(n % 4)
+        peer = ((ray_x + dx) % 4) * 4 + (ray_y + dy) % 4
+        return peer, ((4 - dx) % 4) * 4 + (4 - dy) % 4
 
     def tile_row(m):
         dz, dc = slot_offsets(m)
@@ -80,42 +83,40 @@
     def greet(to_ray, to_brick):
         pl.semaphore_signal(barrier, inc=1, device_id={"ray": to_ray, "brick": to_brick}, device_id_type=MESH)
 
-    for m in range(1, BRICK):
-        greet(ray, (brick + m) % BRICK)
-    for dx, dy in RAY_STEPS:
-        greet(ray_peer(dx, dy), brick)
+    each(BRICK - 1, lambda n: greet(ray, (brick + n + 1) % BRICK))
+    each(RAY - 1, lambda n: greet(ray_step(n)[0], brick))
 
     @pl.when(brick == 0)
     def _():
-        for b in range(BRICK):
-            greet((ray + RAY - 1) % RAY, b)
+        each(BRICK, lambda b: greet((ray + RAY - 1) % RAY, b))
 
     @pl.when(brick == BRICK - 1)
     def _():
-        for b in range(BRICK):
-            greet((ray + 1) % RAY, b)
+        each(BRICK, lambda b: greet((ray + 1) % RAY, b))
 
     load_sino.start()
     load_bundle.start()
 
-    def load_block(m, _):
+    def load_block(m):
         pltpu.make_async_copy(
             blocks_hbm.at[0, pl.ds(2 * tile_row(m), 2)], weights.at[m], weight_sem.at[m]
         ).start()
-        return 0
-
-    lax.fori_loop(0, BRICK, load_block, 0)
+
+    each(BRICK, load_block)
 
     lane = lax.broadcasted_iota(jnp.int32, (8, 128), 1)
     row = lax.broadcasted_iota(jnp.int32, (8, 128), 0)
     lane32 = lax.broadcasted_iota(jnp.int32, (32, 128), 1)
 
     load_est.wait()
-    for s in range(4):
+
+    def lay_out(s):
         even = est[s, pl.ds(0, 32, stride=2), :]
         odd = est[s, pl.ds(1, 32, stride=2), :]
         tmp[pl.ds(s, 32, stride=8), :] = jnp.where(lane32 < 64, even, pltpu.roll(odd, 64, 1))
         tmp[pl.ds(4 + s, 32, stride=8), :] = jnp.where(lane32 < 64, pltpu.roll(even, 64, 1), odd)
+
+    each(4, lay_out)
     tiles[0] = tmp[...].astype(BF).reshape(16, 16, 128)
 
     pl.semaphore_wait(barrier, BRICK - 1 + RAY - 1 + 2)
@@ -137,10 +138,12 @@
     load_sino.wait()
     meta[0, 0:32, :] = sino[...].astype(BF)
     meta[0, 32:48, :] = jnp.concatenate([lane_key, lane_key], axis=0).astype(BF)
-    for dx, dy in RAY_STEPS:
-        remote(
-            meta.at[0], meta.at[ray_slot(dx, dy)], send_sem.at[1], recv_sem.at[1], ray_peer(dx, dy), brick
-        ).start()
+
+    def send_meta(n):
+        peer, slot = ray_step(n)
+        remote(meta.at[0], meta.at[slot], send_sem.at[1], recv_sem.at[1], peer, brick).start()
+
+    each(RAY - 1, send_meta)
 
     above = (brick + BRICK - 1) % BRICK
     above_ray = (ray + (brick + BRICK - 1) // BRICK + RAY - 1) % RAY
@@ -153,7 +156,7 @@
         est.at[:, pl.ds(0, 8), :], est_edges.at[1], send_sem.at[2], recv_sem.at[2], above_ray, above
     ).start()
 
-    def project(m, _):
+    def project(m):
         @pl.when(m > 0)
         def _():
             wait_bytes(tiles.at[m], tile_recv.at[m])
@@ -164,28 +167,36 @@
             remote(tiles.at[m], tiles.at[slot], send_sem.at[0], tile_recv.at[slot], ray, mate).start()
 
         wait_bytes(weights.at[m], weight_sem.at[m])
-        held = tiles[m].astype(F32)
-        left = jnp.concatenate(
-            [half for c in range(16) for half in (held[c, 0:8], held[c, 8:16])], axis=1
-        ).astype(BF)
-        full = lax.dot_general(
-            left, weights[m].reshape(256, 4096), (((1,), (1,)), ((), ())), preferred_element_type=F32
-        )
+
+        def add_columns(n, full):
+            held = tiles[m, pl.ds(4 * n, 4)].astype(F32)
+            left = jnp.concatenate(
+                [half for c in range(4) for half in (held[c, 0:8], held[c, 8:16])], axis=1
+            ).astype(BF)
+            columns = pl.ds(pl.multiple_of(n * 1024, 1024), 1024)
+            return full + lax.dot_general(
+                left, weights[m, :, :, columns].reshape(256, 1024), (((1,), (1,)), ((), ())),
+                preferred_element_type=F32,
+            )
+
+        full = lax.fori_loop(0, 4, add_columns, jnp.zeros((8, 256), F32))
         picked[pl.ds(pl.multiple_of(m * 8, 8), 8), :] = jnp.where(row < 4, full[:, :128], full[:, 128:])
 
         def hand_out(at):
             contrib[0, at, :] = picked[at, :].astype(BF)
-            for dx, dy in RAY_STEPS:
+
+            def send(n):
+                peer, slot = ray_step(n)
                 remote(
-                    contrib.at[0, at], contrib.at[ray_slot(dx, dy), at], send_sem.at[3], recv_sem.at[3],
-                    ray_peer(dx, dy), brick,
+                    contrib.at[0, at], contrib.at[slot, at], send_sem.at[3], recv_sem.at[3], peer, brick
                 ).start()
+
+            each(RAY - 1, send)
 
         pl.when(m == 5)(lambda: hand_out(pl.ds(0, 48)))
         pl.when(m == 7)(lambda: hand_out(pl.ds(48, 16)))
-        return 0
-
-    lax.fori_loop(0, BRICK, project, 0)
+
+    each(BRICK, project)
 
     wait_bytes(meta.at[pl.ds(1, RAY - 1)], recv_sem.at[1])
     own_first = (ray * 32).astype(F32)
@@ -198,20 +209,22 @@
             lane < 64, meta[2 * q, 32:48, :].astype(F32)[0:8], meta[2 * q + 1, 32:48, :].astype(F32)[0:8]
         ) * 4.0 + (lane % 4).astype(F32)
         columns.append(jnp.where(row_keys == jnp.concatenate([key] * 12, axis=0), 1.0, 0.0))
-    row_all = lax.broadcasted_iota(jnp.int32, (96, 128), 0)
+    select = jnp.concatenate(columns, axis=1).astype(BF)
+    sino_columns = []
     for q in range(4):
         owner = ((ray_x + q) % 4) * 4 + (ray_y + lane // 32) % 4
         key = (owner * 32 + lane % 32).astype(F32)
-        hit = (row_keys == jnp.concatenate([key] * 12, axis=0)) & (row_all < 64)
-        columns.append(jnp.where(hit, -1.0, 0.0))
-    select = jnp.concatenate(columns, axis=1).astype(BF)
-    sinos = meta[:, 0:32, :].reshape(512, 128)
+        sino_columns.append(jnp.where(row_keys[0:64] == jnp.concatenate([key] * 8, axis=0), 1.0, 0.0))
+    sino_picked = jnp.dot(
+        jnp.concatenate(sino_columns, axis=1).astype(BF), meta[:, 0:32, :].reshape(512, 128),
+        preferred_element_type=F32,
+    )
+    select_own[...] = select[64:96]
 
     wait_bytes(contrib.at[pl.ds(1, RAY - 1)], recv_sem.at[3])
-    right = jnp.concatenate([contrib[...].reshape(1024, 128), sinos], axis=0)
-    resid = jnp.dot(select, right, preferred_element_type=F32)
-    picked[...] = resid[0:64]
-    res_ref[...] = resid[64:96] - sino[...]
+    picked[...] = (
+        jnp.dot(select[0:64], contrib[...].reshape(1024, 128), preferred_element_type=F32) - sino_picked
+    )
 
     def split_left(m):
         mine = picked[pl.ds(pl.multiple_of(m * 8, 8), 8), :]
@@ -235,31 +248,34 @@
             (ray + (1, RAY - 1)[edge]) % RAY, (0, BRICK - 1)[edge],
         ).start()
 
-    def backproject(t, _):
+    def backproject(t):
         pass_on = (t == 0) | ((t % 2 == 1) & (t < 7))
         g = jnp.where(pass_on, t + 1, t - 1) // 2
         dz, first, stride = ring_step(g)
         dc = jnp.where(pass_on, 1, 0)
         m = first + dc * stride
-        spread = jnp.dot(split_left(m), weights[m].reshape(256, 4096), preferred_element_type=F32)
-        pieces = [
-            jnp.concatenate(
-                [spread[:, c * 256 : c * 256 + 128], spread[:, c * 256 + 128 : c * 256 + 256]], axis=0
+        left = split_left(m)
+
+        def fill(n):
+            columns = pl.ds(pl.multiple_of(n * 1024, 1024), 1024)
+            spread = jnp.dot(
+                left, weights[m, :, :, columns].reshape(256, 1024), preferred_element_type=F32
             )
-            for c in range(16)
-        ]
+            for c in range(4):
+                stage[4 * n + c, 0:8] = spread[:, c * 256 : c * 256 + 128]
+                stage[4 * n + c, 8:16] = spread[:, c * 256 + 128 : c * 256 + 256]
+
+        each(4, fill)
 
         @pl.when(pass_on)
         def _():
-            for c in range(16):
-                mate_out[g, c] = pieces[c].astype(BF)
+            mate_out[g] = stage[...].astype(BF)
             remote(mate_out.at[g], mate_in.at[g], send_sem.at[4], mate_recv.at[g], ray, mate).start()
 
         @pl.when(jnp.logical_not(pass_on))
         def _():
             wait_bytes(mate_in.at[g], mate_recv.at[g])
-            for c in range(16):
-                grad_out[g, c] = (pieces[c] + mate_in[g, c].astype(F32)).astype(BF)
+            grad_out[g] = (stage[...] + mate_in[g].astype(F32)).astype(BF)
             target = ((z + dz) % 4) * 2 + core
 
             @pl.when(g < 3)
@@ -278,9 +294,11 @@
                     grad_out.at[g, 0], halo_low.at[z], send_sem.at[6], recv_sem.at[8], ray, target - 1
                 ).start()
 
-        return 0
-
-    lax.fori_loop(0, BRICK, backproject, 0)
+    each(BRICK, backproject)
+
+    res_ref[...] = (
+        jnp.dot(select_own[...], contrib[...].reshape(1024, 128), preferred_element_type=F32) - sino[...]
+    )
 
     wait_bytes(est_edges, recv_sem.at[2])
     wait_bytes(grad_in, recv_sem.at[5])
@@ -310,11 +328,14 @@
         gathered[272:288, :] = far_in[...].astype(F32).sum(axis=0)
 
     lane36 = lax.broadcasted_iota(jnp.int32, (36, 128), 1)
-    for s in range(4):
+
+    def put_back(s):
         one = gathered[pl.ds(s, 36, stride=8), :]
         two = gathered[pl.ds(4 + s, 36, stride=8), :]
         anchor[s, pl.ds(0, 36, stride=2), :] = jnp.where(lane36 < 64, one, pltpu.roll(two, 64, 1))
         anchor[s, pl.ds(1, 36, stride=2), :] = jnp.where(lane36 < 64, pltpu.roll(one, 64, 1), two)
+
+    each(4, put_back)
     image = jnp.concatenate([est_edges[0, :, 4:8, :], est[...], est_edges[1, :, 0:4, :]], axis=1)
     start = image - step_size * anchor[...]
 
@@ -330,7 +351,7 @@
     wait_bytes(far_out, send_sem.at[7])
 
 
-def sweeps_kernel(start_ref, res_ref, out_hbm, res_hbm, out, save_sem):
+def sweeps_kernel(start_ref, res_ref, out_hbm, res_hbm, out, primal, extra, dual_y, dual_x, dual_z, save_sem):
     ray = lax.axis_index("ray")
     brick = lax.axis_index("brick")
     save_res = pltpu.make_async_copy(res_ref, res_hbm, save_sem.at[0])
@@ -349,27 +370,37 @@
     level = jnp.zeros((1, 72, 128), F32)
 
     start = jnp.where(below_image, 0.0, start_ref[...])
-    primal = start
-    extra = start
-    dual_y = dual_x = dual_z = None
-    for sweep in range(SWEEPS):
-        diff_y = pltpu.roll(extra, 71, 1) - extra
-        diff_x = jnp.where(last_lane, 0.0, pltpu.roll(extra, 127, 2)) - extra
-        diff_z = jnp.concatenate([extra[1:] - extra[:-1], level], axis=0)
-        trial_y, trial_x, trial_z = tv_step * diff_y, tv_step * diff_x, tv_step * diff_z
-        if sweep:
-            trial_y, trial_x, trial_z = dual_y + trial_y, dual_x + trial_x, dual_z + trial_z
+    primal[...] = start
+    extra[...] = start
+    for dual in (dual_y, dual_x, dual_z):
+        dual[...] = jnp.zeros(shape, F32)
+
+    def sweep(n, _):
+        ahead = extra[...]
+        diff_y = pltpu.roll(ahead, 71, 1) - ahead
+        diff_x = jnp.where(last_lane, 0.0, pltpu.roll(ahead, 127, 2)) - ahead
+        diff_z = jnp.concatenate([ahead[1:] - ahead[:-1], level], axis=0)
+        trial_y = dual_y[...] + tv_step * diff_y
+        trial_x = dual_x[...] + tv_step * diff_x
+        trial_z = dual_z[...] + tv_step * diff_z
         norm = trial_y * trial_y + trial_x * trial_x + trial_z * trial_z
         shrink = lax.rsqrt(jnp.maximum(1.0, norm * (1.0 / (tv_weight * tv_weight))))
-        dual_y = jnp.where(above_image, 0.0, trial_y * shrink)
-        dual_x = trial_x * shrink
-        dual_z = trial_z * shrink
-        div = dual_y - pltpu.roll(dual_y, 1, 1)
-        div += dual_x - jnp.where(first_lane, 0.0, pltpu.roll(dual_x, 1, 2))
-        div += dual_z - jnp.concatenate([level, dual_z[:-1]], axis=0)
-        updated = (primal + tv_step * div + tv_step * start) * (1.0 / (1.0 + tv_step))
-        extra = jnp.where(below_image, 0.0, 2.0 * updated - primal)
-        primal = updated
+        new_y = jnp.where(above_image, 0.0, trial_y * shrink)
+        new_x = trial_x * shrink
+        new_z = trial_z * shrink
+        dual_y[...] = new_y
+        dual_x[...] = new_x
+        dual_z[...] = new_z
+        div = new_y - pltpu.roll(new_y, 1, 1)
+        div += new_x - jnp.where(first_lane, 0.0, pltpu.roll(new_x, 1, 2))
+        div += new_z - jnp.concatenate([level, new_z[:-1]], axis=0)
+        before = primal[...]
+        updated = (before + tv_step * div + tv_step * start_ref[...]) * (1.0 / (1.0 + tv_step))
+        extra[...] = jnp.where(below_image, 0.0, 2.0 * updated - before)
+        primal[...] = updated
+        return 0
+
+    lax.fori_loop(0, SWEEPS, sweep, 0)
     out[...] = primal[:, 4:68, :]
     save_out.start()
     save_res.wait()
@@ -397,6 +428,8 @@
             pltpu.VMEM((RAY, 48, 128), BF),
             pltpu.VMEM((RAY, 64, 128), BF),
             pltpu.VMEM((64, 128), F32),
+            pltpu.VMEM((32, 1024), BF),
+            pltpu.VMEM((16, 16, 128), F32),
             pltpu.VMEM((4, 16, 16, 128), BF),
             pltpu.VMEM((4, 16, 16, 128), BF),
             pltpu.VMEM((4, 16, 16, 128), BF),
@@ -427,7 +460,7 @@
         ),
         in_specs=[pl.BlockSpec(memory_space=pltpu.VMEM)] * 2,
         out_specs=(pl.BlockSpec(memory_space=pltpu.HBM),) * 2,
-        scratch_shapes=[pltpu.VMEM((4, 64, 128), F32), dma((2,))],
+        scratch_shapes=[pltpu.VMEM((4, 64, 128), F32)] + [pltpu.VMEM((4, 72, 128), F32)] * 5 + [dma((2,))],
         compiler_params=pltpu.CompilerParams(vmem_limit_bytes=16 * 1024 * 1024),
     )(start, residual)
     return restored, residual.reshape(sinogram.shape)

time: 31.6 us -> 36.9 us (1.17)
  Pallas kernels: 30.8 us -> 36.2 us
    pallas_call x1, Pallas kernels: 29.5 us -> 34.8 us  [shards(): pl.pallas_call(kernel, out_shape=(jax.ShapeDtypeStruct((4, 72, 128), F32)...]
where the time goes in v5:
time: 36.9 us; the launch traced here: 36.8 us
  Pallas kernels  36.2 us (98%)
  between operations  0.64 us (2%)
    pallas_call x1, Pallas kernels, shards(): pl.pallas_call(kernel, out_shape=(jax.ShapeDtypeStruct((4, 72, 128), F32)...  34.8 us
    pallas_call x1, Pallas kernels, shards(): pl.pallas_call(sweeps_kernel, out_shape=(jax.ShapeDtypeStruct((4, 64, 128...  1.44 us

profile of v5, /device:TPU:1, one launch (start us, length us, event | category | flops | bytes accessed | tf_op | source)
XLA Modules:
  0.0 36.8 jit_solution(8883915294638894705)
XLA Ops:
  0.6 34.8 %shard_map.59 = (f32[4,72,128]{2,1,0:T(8,128)S(1)}, f32[32,128]{1,0:T(8,128)S(1)}) custom-call(f32[4,64,128]{2,1,0:T(8,128)} %est_hbm.1, bf16[1,16,128,4096]{3,2,1,0:T(8,128)(2,1)} %blocks_hbm.1, s32[1,16]{1,0:T(1,128)} %bundle_hbm.1, f32[32,128]{1,0:T(8,128)} %bitcast.2), custom_call_target="tpu_custom_call" | custom-call | tf_op jit(solution)/shard_map/pallas_call | solution.py:413
  35.4 1.4 %shard_map.60 = (f32[4,64,128]{2,1,0:T(8,128)}, f32[32,128]{1,0:T(8,128)}) custom-call(f32[4,72,128]{2,1,0:T(8,128)S(1)} %get-tuple-element.6.start_ref, f32[32,128]{1,0:T(8,128)S(1)} %get-tuple-element.7.res_ref), custom_call_target="tpu_custom_call" | custom-call | tf_op jit(solution)/shard_map/pallas_call | solution.py:455

commit v6 on v4

--- a/solution.py
+++ b/solution.py
@@ -41,7 +41,7 @@
 def kernel(
     est_hbm, blocks_hbm, bundle_hbm, sino_hbm,
     out_ref, res_ref,
-    bundles, est, sino, tiles, tmp, weights, meta, contrib, picked, mate_out, mate_in, grad_out, grad_in,
+    bundles, est, sino, tiles, tmp, weights, meta, contrib, picked, select_own, mate_out, mate_in, grad_out, grad_in,
     halo_top, halo_low, far_out, far_in, est_edges, gathered, anchor,
     load_sem, weight_sem, tile_recv, mate_recv, send_sem, recv_sem,
 ):
@@ -198,20 +198,22 @@
             lane < 64, meta[2 * q, 32:48, :].astype(F32)[0:8], meta[2 * q + 1, 32:48, :].astype(F32)[0:8]
         ) * 4.0 + (lane % 4).astype(F32)
         columns.append(jnp.where(row_keys == jnp.concatenate([key] * 12, axis=0), 1.0, 0.0))
-    row_all = lax.broadcasted_iota(jnp.int32, (96, 128), 0)
+    select = jnp.concatenate(columns, axis=1).astype(BF)
+    sino_columns = []
     for q in range(4):
         owner = ((ray_x + q) % 4) * 4 + (ray_y + lane // 32) % 4
         key = (owner * 32 + lane % 32).astype(F32)
-        hit = (row_keys == jnp.concatenate([key] * 12, axis=0)) & (row_all < 64)
-        columns.append(jnp.where(hit, -1.0, 0.0))
-    select = jnp.concatenate(columns, axis=1).astype(BF)
-    sinos = meta[:, 0:32, :].reshape(512, 128)
+        sino_columns.append(jnp.where(row_keys[0:64] == jnp.concatenate([key] * 8, axis=0), 1.0, 0.0))
+    sino_picked = jnp.dot(
+        jnp.concatenate(sino_columns, axis=1).astype(BF), meta[:, 0:32, :].reshape(512, 128),
+        preferred_element_type=F32,
+    )
+    select_own[...] = select[64:96]
 
     wait_bytes(contrib.at[pl.ds(1, RAY - 1)], recv_sem.at[3])
-    right = jnp.concatenate([contrib[...].reshape(1024, 128), sinos], axis=0)
-    resid = jnp.dot(select, right, preferred_element_type=F32)
-    picked[...] = resid[0:64]
-    res_ref[...] = resid[64:96] - sino[...]
+    picked[...] = (
+        jnp.dot(select[0:64], contrib[...].reshape(1024, 128), preferred_element_type=F32) - sino_picked
+    )
 
     def split_left(m):
         mine = picked[pl.ds(pl.multiple_of(m * 8, 8), 8), :]
@@ -219,25 +221,26 @@
             [jnp.where(row < 4, mine, 0.0), jnp.where(row < 4, 0.0, mine)], axis=1
         ).astype(BF)
 
-    for edge, (last, column) in enumerate(((BRICK - 1, 15), (0, 0))):
-        dz = (last // 2 + 4 - z) % 4
-        dc = (last + core) % 2
-        odd = dz % 2
-        m = odd * (2 + dz // 2 + 2 * dc) + (1 - odd) * (3 * dz + dc)
-        rim = jnp.dot(
-            split_left(m),
-            weights[m, :, :, column * 256 : column * 256 + 256].reshape(256, 256),
-            preferred_element_type=F32,
-        )
-        far_out[edge] = jnp.concatenate([rim[:, :128], rim[:, 128:]], axis=0).astype(BF)
-        remote(
-            far_out.at[edge], far_in.at[brick], send_sem.at[7], recv_sem.at[7],
-            (ray + (1, RAY - 1)[edge]) % RAY, (0, BRICK - 1)[edge],
-        ).start()
+    def send_far():
+        for edge, (last, column) in enumerate(((BRICK - 1, 15), (0, 0))):
+            dz = (last // 2 + 4 - z) % 4
+            dc = (last + core) % 2
+            odd = dz % 2
+            m = odd * (2 + dz // 2 + 2 * dc) + (1 - odd) * (3 * dz + dc)
+            rim = jnp.dot(
+                split_left(m),
+                weights[m, :, :, column * 256 : column * 256 + 256].reshape(256, 256),
+                preferred_element_type=F32,
+            )
+            far_out[edge] = jnp.concatenate([rim[:, :128], rim[:, 128:]], axis=0).astype(BF)
+            remote(
+                far_out.at[edge], far_in.at[brick], send_sem.at[7], recv_sem.at[7],
+                (ray + (1, RAY - 1)[edge]) % RAY, (0, BRICK - 1)[edge],
+            ).start()
 
     def backproject(t, _):
-        pass_on = (t == 0) | ((t % 2 == 1) & (t < 7))
-        g = jnp.where(pass_on, t + 1, t - 1) // 2
+        pass_on = (t == 0) | (t == 1) | (t == 3) | (t == 6)
+        g = jnp.where(pass_on, (t + 1) // 2, jnp.where(t == 5, 2, (t - 1) // 2))
         dz, first, stride = ring_step(g)
         dc = jnp.where(pass_on, 1, 0)
         m = first + dc * stride
@@ -254,6 +257,7 @@
             for c in range(16):
                 mate_out[g, c] = pieces[c].astype(BF)
             remote(mate_out.at[g], mate_in.at[g], send_sem.at[4], mate_recv.at[g], ray, mate).start()
+            pl.when(t == 1)(send_far)
 
         @pl.when(jnp.logical_not(pass_on))
         def _():
@@ -281,6 +285,10 @@
         return 0
 
     lax.fori_loop(0, BRICK, backproject, 0)
+
+    res_ref[...] = (
+        jnp.dot(select_own[...], contrib[...].reshape(1024, 128), preferred_element_type=F32) - sino[...]
+    )
 
     wait_bytes(est_edges, recv_sem.at[2])
     wait_bytes(grad_in, recv_sem.at[5])
@@ -397,6 +405,7 @@
             pltpu.VMEM((RAY, 48, 128), BF),
             pltpu.VMEM((RAY, 64, 128), BF),
             pltpu.VMEM((64, 128), F32),
+            pltpu.VMEM((32, 1024), BF),
             pltpu.VMEM((4, 16, 16, 128), BF),
             pltpu.VMEM((4, 16, 16, 128), BF),
             pltpu.VMEM((4, 16, 16, 128), BF),

time: 31.6 us -> 31.2 us (0.987)
    pallas_call x1, Pallas kernels: 29.5 us -> 29.1 us  [shards(): pl.pallas_call(kernel, out_shape=(jax.ShapeDtypeStruct((4, 72, 128), F32)...]
where the time goes in v6:
time: 31.2 us; the launch traced here: 31.1 us
  Pallas kernels  30.5 us (98%)
  between operations  0.64 us (2%)
    pallas_call x1, Pallas kernels, shards(): pl.pallas_call(kernel, out_shape=(jax.ShapeDtypeStruct((4, 72, 128), F32)...  29.1 us
    pallas_call x1, Pallas kernels, shards(): pl.pallas_call(sweeps_kernel, out_shape=(jax.ShapeDtypeStruct((4, 64, 128...  1.32 us

profile of v6, /device:TPU:1, one launch (start us, length us, event | category | flops | bytes accessed | tf_op | source)
XLA Modules:
  0.0 31.1 jit_solution(1446082983744965779)
XLA Ops:
  0.6 29.1 %shard_map.59 = (f32[4,72,128]{2,1,0:T(8,128)S(1)}, f32[32,128]{1,0:T(8,128)S(1)}) custom-call(f32[4,64,128]{2,1,0:T(8,128)} %est_hbm.1, bf16[1,16,128,4096]{3,2,1,0:T(8,128)(2,1)} %blocks_hbm.1, s32[1,16]{1,0:T(1,128)} %bundle_hbm.1, f32[32,128]{1,0:T(8,128)} %bitcast.2), custom_call_target="tpu_custom_call" | custom-call | tf_op jit(solution)/shard_map/pallas_call | solution.py:390
  29.8 1.3 %shard_map.60 = (f32[4,64,128]{2,1,0:T(8,128)}, f32[32,128]{1,0:T(8,128)}) custom-call(f32[4,72,128]{2,1,0:T(8,128)S(1)} %get-tuple-element.6.start_ref, f32[32,128]{1,0:T(8,128)S(1)} %get-tuple-element.7.res_ref), custom_call_target="tpu_custom_call" | custom-call | tf_op jit(solution)/shard_map/pallas_call | solution.py:431

commit v7 on v6

--- a/solution.py
+++ b/solution.py
@@ -43,7 +43,7 @@
     out_ref, res_ref,
     bundles, est, sino, tiles, tmp, weights, meta, contrib, picked, select_own, mate_out, mate_in, grad_out, grad_in,
     halo_top, halo_low, far_out, far_in, est_edges, gathered, anchor,
-    load_sem, weight_sem, tile_recv, mate_recv, send_sem, recv_sem,
+    line_sem, load_sem, weight_sem, tile_recv, mate_recv, send_sem, recv_sem,
 ):
     ray = lax.axis_index("ray")
     brick = lax.axis_index("brick")
@@ -82,18 +82,9 @@
 
     for m in range(1, BRICK):
         greet(ray, (brick + m) % BRICK)
-    for dx, dy in RAY_STEPS:
-        greet(ray_peer(dx, dy), brick)
-
-    @pl.when(brick == 0)
-    def _():
-        for b in range(BRICK):
-            greet((ray + RAY - 1) % RAY, b)
-
-    @pl.when(brick == BRICK - 1)
-    def _():
-        for b in range(BRICK):
-            greet((ray + 1) % RAY, b)
+    for d in range(1, 4):
+        greet(ray_peer(d, 0), brick)
+        greet(ray_peer(0, d), brick)
 
     load_sino.start()
     load_bundle.start()
@@ -118,12 +109,17 @@
         tmp[pl.ds(4 + s, 32, stride=8), :] = jnp.where(lane32 < 64, pltpu.roll(even, 64, 1), odd)
     tiles[0] = tmp[...].astype(BF).reshape(16, 16, 128)
 
-    pl.semaphore_wait(barrier, BRICK - 1 + RAY - 1 + 2)
+    pl.semaphore_wait(barrier, BRICK - 1 + 6)
 
     remote(tiles.at[0], tiles.at[1], send_sem.at[0], tile_recv.at[1], ray, mate).start()
     for step, slot in ((1, 2), (3, 3), (2, 6)):
         to = ((z + 4 - step) % 4) * 2 + core
         remote(tiles.at[0], tiles.at[slot], send_sem.at[0], tile_recv.at[slot], ray, to).start()
+
+    for d in range(1, 4):
+        pl.semaphore_signal(
+            line_sem, inc=1, device_id={"ray": ray_peer(d, 0), "brick": brick}, device_id_type=MESH
+        )
 
     load_bundle.wait()
     row_keys = []
@@ -137,21 +133,12 @@
     load_sino.wait()
     meta[0, 0:32, :] = sino[...].astype(BF)
     meta[0, 32:48, :] = jnp.concatenate([lane_key, lane_key], axis=0).astype(BF)
-    for dx, dy in RAY_STEPS:
-        remote(
-            meta.at[0], meta.at[ray_slot(dx, dy)], send_sem.at[1], recv_sem.at[1], ray_peer(dx, dy), brick
-        ).start()
-
-    above = (brick + BRICK - 1) % BRICK
-    above_ray = (ray + (brick + BRICK - 1) // BRICK + RAY - 1) % RAY
-    below = (brick + 1) % BRICK
-    below_ray = (ray + (brick + 1) // BRICK) % RAY
-    remote(
-        est.at[:, pl.ds(56, 8), :], est_edges.at[0], send_sem.at[2], recv_sem.at[2], below_ray, below
-    ).start()
-    remote(
-        est.at[:, pl.ds(0, 8), :], est_edges.at[1], send_sem.at[2], recv_sem.at[2], above_ray, above
-    ).start()
+    def send_meta():
+        pl.semaphore_wait(line_sem, 3)
+        for dx, dy in RAY_STEPS:
+            remote(
+                meta.at[0], meta.at[ray_slot(dx, dy)], send_sem.at[1], recv_sem.at[1], ray_peer(dx, dy), brick
+            ).start()
 
     def project(m, _):
         @pl.when(m > 0)
@@ -181,6 +168,7 @@
                     ray_peer(dx, dy), brick,
                 ).start()
 
+        pl.when(m == 1)(send_meta)
         pl.when(m == 5)(lambda: hand_out(pl.ds(0, 48)))
         pl.when(m == 7)(lambda: hand_out(pl.ds(48, 16)))
         return 0
@@ -214,6 +202,17 @@
     picked[...] = (
         jnp.dot(select[0:64], contrib[...].reshape(1024, 128), preferred_element_type=F32) - sino_picked
     )
+
+    above = (brick + BRICK - 1) % BRICK
+    above_ray = (ray + (brick + BRICK - 1) // BRICK + RAY - 1) % RAY
+    below = (brick + 1) % BRICK
+    below_ray = (ray + (brick + 1) // BRICK) % RAY
+    remote(
+        est.at[:, pl.ds(56, 8), :], est_edges.at[0], send_sem.at[2], recv_sem.at[2], below_ray, below
+    ).start()
+    remote(
+        est.at[:, pl.ds(0, 8), :], est_edges.at[1], send_sem.at[2], recv_sem.at[2], above_ray, above
+    ).start()
 
     def split_left(m):
         mine = picked[pl.ds(pl.multiple_of(m * 8, 8), 8), :]
@@ -417,6 +416,7 @@
             pltpu.VMEM((2, 4, 8, 128), F32),
             pltpu.VMEM((288, 128), F32),
             pltpu.VMEM((4, 72, 128), F32),
+            pltpu.SemaphoreType.REGULAR,
             dma((3,)),
             dma((BRICK,)),
             dma((BRICK,)),

time: 31.2 us -> 30.7 us (0.984)
  Pallas kernels: 30.5 us -> 30 us
    pallas_call x1, Pallas kernels: 29.1 us -> 28.7 us  [shards(): pl.pallas_call(kernel, out_shape=(jax.ShapeDtypeStruct((4, 72, 128), F32)...]
where the time goes in v7:
time: 30.7 us; the launch traced here: 30.6 us
  Pallas kernels  30 us (98%)
  between operations  0.64 us (2%)
    pallas_call x1, Pallas kernels, shards(): pl.pallas_call(kernel, out_shape=(jax.ShapeDtypeStruct((4, 72, 128), F32)...  28.7 us
    pallas_call x1, Pallas kernels, shards(): pl.pallas_call(sweeps_kernel, out_shape=(jax.ShapeDtypeStruct((4, 64, 128...  1.32 us

profile of v7, /device:TPU:1, one launch (start us, length us, event | category | flops | bytes accessed | tf_op | source)
XLA Modules:
  0.0 30.6 jit_solution(7166896403329747432)
XLA Ops:
  0.6 28.7 %shard_map.59 = (f32[4,72,128]{2,1,0:T(8,128)S(1)}, f32[32,128]{1,0:T(8,128)S(1)}) custom-call(f32[4,64,128]{2,1,0:T(8,128)} %est_hbm.1, bf16[1,16,128,4096]{3,2,1,0:T(8,128)(2,1)} %blocks_hbm.1, s32[1,16]{1,0:T(1,128)} %bundle_hbm.1, f32[32,128]{1,0:T(8,128)} %bitcast.2), custom_call_target="tpu_custom_call" | custom-call | tf_op jit(solution)/shard_map/pallas_call | solution.py:389
  29.3 1.3 %shard_map.60 = (f32[4,64,128]{2,1,0:T(8,128)}, f32[32,128]{1,0:T(8,128)}) custom-call(f32[4,72,128]{2,1,0:T(8,128)S(1)} %get-tuple-element.6.start_ref, f32[32,128]{1,0:T(8,128)S(1)} %get-tuple-element.7.res_ref), custom_call_target="tpu_custom_call" | custom-call | tf_op jit(solution)/shard_map/pallas_call | solution.py:431

commit v8 on v7

--- a/solution.py
+++ b/solution.py
@@ -80,8 +80,9 @@
     def greet(to_ray, to_brick):
         pl.semaphore_signal(barrier, inc=1, device_id={"ray": to_ray, "brick": to_brick}, device_id_type=MESH)
 
-    for m in range(1, BRICK):
-        greet(ray, (brick + m) % BRICK)
+    greet(ray, mate)
+    for d in range(1, 4):
+        greet(ray, (brick + 2 * d) % BRICK)
     for d in range(1, 4):
         greet(ray_peer(d, 0), brick)
         greet(ray_peer(0, d), brick)
@@ -89,13 +90,6 @@
     load_sino.start()
     load_bundle.start()
 
-    def load_block(m, _):
-        pltpu.make_async_copy(
-            blocks_hbm.at[0, pl.ds(2 * tile_row(m), 2)], weights.at[m], weight_sem.at[m]
-        ).start()
-        return 0
-
-    lax.fori_loop(0, BRICK, load_block, 0)
 
     lane = lax.broadcasted_iota(jnp.int32, (8, 128), 1)
     row = lax.broadcasted_iota(jnp.int32, (8, 128), 0)
@@ -109,12 +103,20 @@
         tmp[pl.ds(4 + s, 32, stride=8), :] = jnp.where(lane32 < 64, pltpu.roll(even, 64, 1), odd)
     tiles[0] = tmp[...].astype(BF).reshape(16, 16, 128)
 
-    pl.semaphore_wait(barrier, BRICK - 1 + 6)
+    pl.semaphore_wait(barrier, 4 + 6)
 
     remote(tiles.at[0], tiles.at[1], send_sem.at[0], tile_recv.at[1], ray, mate).start()
     for step, slot in ((1, 2), (3, 3), (2, 6)):
         to = ((z + 4 - step) % 4) * 2 + core
         remote(tiles.at[0], tiles.at[slot], send_sem.at[0], tile_recv.at[slot], ray, to).start()
+
+    def load_block(m, _):
+        pltpu.make_async_copy(
+            blocks_hbm.at[0, pl.ds(2 * tile_row(m), 2)], weights.at[m], weight_sem.at[m]
+        ).start()
+        return 0
+
+    lax.fori_loop(0, BRICK, load_block, 0)
 
     for d in range(1, 4):
         pl.semaphore_signal(

time: 30.7 us -> 31 us (level)
  no operation moved by 1% of the time
where the time goes in v8:
time: 31 us; the launch traced here: 30.8 us
  Pallas kernels  30.2 us (97%)
  between operations  0.64 us (2%)
    pallas_call x1, Pallas kernels, shards(): pl.pallas_call(kernel, out_shape=(jax.ShapeDtypeStruct((4, 72, 128), F32)...  28.9 us
    pallas_call x1, Pallas kernels, shards(): pl.pallas_call(sweeps_kernel, out_shape=(jax.ShapeDtypeStruct((4, 64, 128...  1.32 us

profile of v8, /device:TPU:1, one launch (start us, length us, event | category | flops | bytes accessed | tf_op | source)
XLA Modules:
  0.0 30.8 jit_solution(3271867353230964450)
XLA Ops:
  0.6 28.9 %shard_map.59 = (f32[4,72,128]{2,1,0:T(8,128)S(1)}, f32[32,128]{1,0:T(8,128)S(1)}) custom-call(f32[4,64,128]{2,1,0:T(8,128)} %est_hbm.1, bf16[1,16,128,4096]{3,2,1,0:T(8,128)(2,1)} %blocks_hbm.1, s32[1,16]{1,0:T(1,128)} %bundle_hbm.1, f32[32,128]{1,0:T(8,128)} %bitcast.2), custom_call_target="tpu_custom_call" | custom-call | tf_op jit(solution)/shard_map/pallas_call | solution.py:391
  29.5 1.3 %shard_map.60 = (f32[4,64,128]{2,1,0:T(8,128)}, f32[32,128]{1,0:T(8,128)}) custom-call(f32[4,72,128]{2,1,0:T(8,128)S(1)} %get-tuple-element.6.start_ref, f32[32,128]{1,0:T(8,128)S(1)} %get-tuple-element.7.res_ref), custom_call_target="tpu_custom_call" | custom-call | tf_op jit(solution)/shard_map/pallas_call | solution.py:433
